TPU v7x, 256 devices: a whole 4x4x8 slice. The times are simulated.
256 devices in a mesh: video: 4 (over z_lo), slab: 64 (over y, x, z_hi, core).
Axes of the slice: x: 4, y: 4, z: 8 (z_hi: 2, z_lo: 4; z = z_hi * 4 + z_lo), core: 2. Of those that a mesh axis runs over, the one named last changes fastest.
Arguments:
- section_input: bfloat16 [24, 96, 256, 128], P('video', None, 'slab'), parts along dimension 0, may hold values from -6 to 6
- main_cache: bfloat16 [8, 96, 256, 128], P('video', None, 'slab'), parts along dimension 0, may hold values from -5 to 5
- head_cache: bfloat16 [8, 96, 256, 128], P('video', None, 'slab'), parts along dimension 0, may hold values from -5 to 5
- gain_in: float32 [96], replicated, may hold values from 0.25 to 1.75
- gain_out: float32 [96], replicated, may hold values from 0.25 to 1.75
- main_weight: bfloat16 [3, 3, 3, 96, 96], replicated, may hold values from -0.125 to 0.125
- head_weight: bfloat16 [3, 3, 3, 3, 96], replicated, may hold values from -0.125 to 0.125
- aspect_grad: bfloat16 [24, 4, 256, 128], P('video', None, 'slab'), parts along dimension 0, may hold values from -6 to 6
- aspect_table: float32 [16, 3, 4], replicated, may hold values from -4 to 4
- aspect_index: int32 [24], P('video'), parts along dimension 0, may hold values from 0 to 15
- frame_order: int32 [6], replicated, may hold values from 0 to 5, each once
Outputs:
- grad_input: float32 [24, 96, 256, 128], P('video', None, 'slab'), parts along dimension 0
- grad_main_weight: float32 [12, 3, 3, 96, 96], P('video'), parts along dimension 0
- grad_head_weight: float32 [12, 3, 3, 3, 96], P('video'), parts along dimension 0
There are 4 independent parts, one for each index of `video`. A program takes and returns all parts, laid end to end along the dimension named above; an argument that names none is the same for every part. Nothing has to cross between parts.
All inputs are finite; a program needn't handle non-finite values.
Results may differ from a plain program's by a relative error of at most 0.015.
Values may be sent and summed in bfloat16 or wider, within the bound.
A program may use at most 128 MiB of HBM per device.

v0:
```python
import jax
import jax.numpy as jnp
from jax import lax
from jax.sharding import PartitionSpec as P

EPS = 1e-06


def padded_2(value, sides, width):
    for axis, dim in sides:
        size, length = (lax.axis_size(axis), value.shape[dim])
        up = [(i, (i + 1) % size) for i in range(size - 1)]
        down = [(j, i) for i, j in up]
        last = lax.slice_in_dim(value, length - width, length, axis=dim)
        initial = lax.slice_in_dim(value, 0, width, axis=dim)
        before = lax.ppermute(last, axis, up)
        after = lax.ppermute(initial, axis, down)
        value = jnp.concatenate([before, value, after], axis=dim)
    return value


def norm_silu(value, gain):
    meansq = jnp.mean(value * value, axis=1, keepdims=True)
    normed = value * lax.rsqrt(meansq + EPS) * gain[None, :, None, None]
    return normed * jax.nn.sigmoid(normed)


def widen(field):
    return jnp.pad(field, ((0, 0), (0, 0), (0, 0), (1, 1)))


def patches(padded, rows, cols):
    parts = [padded[:, :, y : y + rows, x : x + cols] for y in range(3) for x in range(3)]
    return jnp.concatenate(parts, axis=1)


def conv_forward(padded, weight, frames, rows):
    cols = padded.shape[3] - 2
    total = None
    for t in range(3):
        flat = jnp.transpose(weight[t], (2, 0, 1, 3)).reshape(weight.shape[3], -1)
        stack = patches(padded[t : t + frames], rows, cols)
        term = jnp.einsum("ok,fkhw->fohw", flat, stack, preferred_element_type=jnp.float32)
        total = term if total is None else total + term
    return total


def conv_transpose(grad_pad, weight, rows):
    frames = grad_pad.shape[0]
    cols = grad_pad.shape[3] - 2
    parts = [
        grad_pad[:, :, 2 - y : 2 - y + rows, 2 - x : 2 - x + cols]
        for y in range(3)
        for x in range(3)
    ]
    stack = jnp.concatenate(parts, axis=1)
    full = jnp.zeros((frames + 2, weight.shape[4], rows, cols), jnp.float32)
    for t in range(3):
        flat = weight[t].reshape(-1, weight.shape[4])
        term = jnp.einsum("kc,fkhw->fchw", flat, stack, preferred_element_type=jnp.float32)
        full = full.at[t : t + frames].add(term)
    return full[2:]


def weight_grad(grad, padded, rows):
    frames = grad.shape[0]
    cols = padded.shape[3] - 2
    result = []
    for t in range(3):
        stack = patches(padded[t : t + frames], rows, cols)
        flat = jnp.einsum("fohw,fkhw->ok", grad, stack, preferred_element_type=jnp.float32)
        shaped = flat.reshape(grad.shape[1], 3, 3, padded.shape[1])
        result.append(jnp.transpose(shaped, (1, 2, 0, 3)))
    return jnp.stack(result, 0)


def local(
    section_input,
    main_cache,
    head_cache,
    gain_in,
    gain_out,
    main_weight,
    head_weight,
    aspect_grad,
    aspect_table,
    aspect_index,
    frame_order,
):
    frames, chans, rows, cols = section_input.shape
    slabs = lax.axis_size("slab")
    xfloat = section_input.astype(jnp.float32)
    hidden = norm_silu(xfloat, gain_in).astype(jnp.bfloat16)
    hin_rim = padded_2(jnp.concatenate([main_cache, hidden], 0), (("slab", 2),), 1)
    hin_pad = widen(hin_rim)
    out = xfloat + conv_forward(hin_pad, main_weight, frames, rows)
    head_hidden = norm_silu(out, gain_out).astype(jnp.bfloat16)
    head_rim_rows = padded_2(jnp.concatenate([head_cache, head_hidden], 0), (("slab", 2),), 1)
    head_pad = widen(head_rim_rows)
    owner = (frame_order[None, :] == jnp.arange(frames, dtype=jnp.int32)[:, None]).astype(
        jnp.float32
    )
    picked = (
        aspect_index[:, None] == jnp.arange(aspect_table.shape[0], dtype=jnp.int32)[None, :]
    ).astype(jnp.float32)
    coeff = jnp.einsum("fn,nca->fca", picked, aspect_table)
    pixel_grad = jnp.einsum(
        "fj,fca,jahw->fchw", owner, coeff, aspect_grad.astype(jnp.float32)
    ).astype(jnp.bfloat16)
    signal_pad = widen(padded_2(pixel_grad, (("slab", 2),), 1))
    d_hh = conv_transpose(signal_pad, head_weight, rows)
    head_part = weight_grad(pixel_grad, head_pad, rows)
    _, pull_out = jax.vjp(lambda value: norm_silu(value, gain_out), out)
    d_out = pull_out(d_hh)[0]
    d_out_b = d_out.astype(jnp.bfloat16)
    grad_pad = widen(padded_2(d_out_b, (("slab", 2),), 1))
    d_hidden = conv_transpose(grad_pad, main_weight, rows)
    main_part = weight_grad(d_out_b, hin_pad, rows)
    main_sum, head_sum = lax.psum((main_part, head_part), "slab")
    _, pull_in = jax.vjp(lambda value: norm_silu(value, gain_in), xfloat)
    grad_input = d_out + pull_in(d_hidden)[0]
    scale = 1.0 / jnp.sqrt(jnp.float32(frames * rows * slabs * cols))
    return (grad_input, main_sum * scale, head_sum * scale)


def solution(mesh):
    placed = (
        P("video", None, "slab", None),
        P("video", None, "slab", None),
        P("video", None, "slab", None),
        P(),
        P(),
        P(),
        P(),
        P("video", None, "slab", None),
        P(),
        P("video"),
        P(),
    )
    return jax.shard_map(
        local,
        mesh=mesh,
        in_specs=placed,
        out_specs=(
            P("video", None, "slab", None),
            P("video", None, None, None, None),
            P("video", None, None, None, None),
        ),
        check_vma=False,
    )
```

profile of v0, /device:TPU:1, one launch (start us, length us, event | category | flops | bytes accessed | tf_op | source)
XLA Modules:
  0.0 879.4 jit_solution(17116502782044544122)
XLA Ops:
  9.5 1.5 fusion.33
  11.7 5.1 collective-permute-start.3
  16.9 7.0 collective-permute-start.2
  25.8 2.4 collective-permute-start
  28.2 1.9 collective-permute-start.1
  32.2 5.1 collective-permute-done.1
  39.2 1.8 select_maximum_fusion.3
  51.6 1.5 fusion.73
  53.1 1.9 collective-permute-start.5
  55.1 7.7 collective-permute-start.4
  62.8 1.5 fusion.72
  70.2 1.6 fusion.34
  72.7 1.9 collective-permute-start.7
  74.6 8.6 collective-permute-start.6
  83.3 1.5 fusion.71
  86.0 1.8 copy.48
  87.7 1.8 select_maximum_fusion
  94.6 2.2 copy-done.3
  98.6 1.5 convolution_bitcast_fusion.6
  100.2 4.0 convolution_bitcast_fusion.7
  104.3 4.0 convolution_bitcast_fusion.8
  108.4 395.6 %psum.15 = f32[3,3,3,3,96]{4,3,2,1,0:T(4,128)S(1)} all-reduce(f32[3,3,3,3,96]{4,3,2,1,0:T(4,128)S(1)} %pad_maximum_fusion.7), channel_id=1, replica_groups=mesh['video'=4,'slab'=64] {'slab'}, use_global_device_ids=true, to_apply=%region_5.6 | all-reduce | flops 7776 | bytes 62208 | tf_op jit(solution)/shard_map/psum | solution.py:119
  504.7 364.9 %all-reduce.8.cloned.1.call-done = f32[3,3,3,96,96]{3,4,2,1,0:T(8,128)} async-done(((f32[3,3,3,96,96]{3,4,2,1,0:T(8,128)}), f32[3,3,3,96,96]{3,4,2,1,0:T(8,128)}) %all-reduce.8.cloned.1.call-update) | async-done | bytes 995344 | tf_op jit(solution)/shard_map/psum | solution.py:119
  871.0 1.5 copy.49
  (112 shorter events, 36.1 us)
Async XLA Ops:
  7.2 17.7 %copy-start = (bf16[6,4,4,128]{3,2,1,0:T(4,128)(2,1)S(1)}, bf16[6,4,4,128]{3,2,1,0:T(4,128)(2,1)}, u32[]{:S(2)}) copy-start(bf16[6,4,4,128]{3,2,1,0:T(4,128)(2,1)} %param.30) | copy-start | bytes 73732
  7.2 24.3 %copy-start.6 = (bf16[3,3,3,3,96]{4,3,2,1,0:T(4,128)(2,1)S(1)}, bf16[3,3,3,3,96]{4,3,2,1,0:T(4,128)(2,1)}, u32[]{:S(2)}) copy-start(bf16[3,3,3,3,96]{4,3,2,1,0:T(4,128)(2,1)} %param.29) | copy-start | bytes 46660
  7.2 24.9 %copy-start.5 = (bf16[2,96,4,128]{3,2,1,0:T(4,128)(2,1)S(1)}, bf16[2,96,4,128]{3,2,1,0:T(4,128)(2,1)}, u32[]{:S(2)}) copy-start(bf16[2,96,4,128]{3,2,1,0:T(4,128)(2,1)} %param.25) | copy-start | bytes 589828
  7.2 862.4 %all-reduce.8.cloned.1.call-start = ((), (), s32[]{:S(2)}) async-start(), calls=%async_computation | async-start | bytes 2654208 | tf_op jit(solution)/shard_map/psum | solution.py:119
  11.7 27.5 %collective-permute-start.3 = (bf16[8,96,1,128]{3,1,2,0:T(8,128)(2,1)}, bf16[8,96,1,128]{3,1,2,0:T(8,128)(2,1)S(1)}, u32[]{:S(2)}, u32[]{:S(2)}) collective-permute-start(bf16[8,96,1,128]{3,1,2,0:T(8,128)(2,1)} %get-tuple-element.136), channel_id=1, source_target_pairs={{1,0},{2,1},{3,2},{4,3},{5,4},{6,5},{7,6},{8,7},{9,8},{10,9},{11,1... | collective-permute-start | bytes 589832 | tf_op jit(solution)/shard_map/ppermute | solution.py:17
  16.9 22.4 %collective-permute-start.2 = (bf16[8,96,1,128]{3,1,2,0:T(8,128)(2,1)S(1)}, bf16[8,96,1,128]{3,1,2,0:T(8,128)(2,1)S(1)}, u32[]{:S(2)}, u32[]{:S(2)}) collective-permute-start(bf16[8,96,1,128]{3,1,2,0:T(8,128)(2,1)S(1)} %get-tuple-element.135), channel_id=1, source_target_pairs={{0,1},{1,2},{2,3},{3,4},{4,5},{5,6},{6,7},{7,8},{8,9},{9,10},{10,1... | collective-permute-start | bytes 589832 | tf_op jit(solution)/shard_map/ppermute | solution.py:16
  25.8 6.4 collective-permute-start
  28.2 9.1 %collective-permute-start.1 = (bf16[6,3,1,128]{3,1,2,0:T(4,128)(2,1)S(1)}, bf16[6,3,1,128]{3,1,2,0:T(4,128)(2,1)S(1)}, u32[]{:S(2)}, u32[]{:S(2)}) collective-permute-start(bf16[6,3,1,128]{3,1,2,0:T(4,128)(2,1)S(1)} %get-tuple-element.157), channel_id=1, source_target_pairs={{1,0},{2,1},{3,2},{4,3},{5,4},{6,5},{7,6},{8,7},{9,8},{10,9},{11,1... | collective-permute-start | bytes 13832 | tf_op jit(solution)/shard_map/ppermute | solution.py:17
  42.6 1.7 copy-start.2
  42.6 1.7 copy-start.7
  49.1 1.2 copy-start.8
  53.1 11.2 %collective-permute-start.5 = (bf16[6,96,1,128]{3,1,2,0:T(8,128)(2,1)S(1)}, bf16[6,96,1,128]{3,1,2,0:T(8,128)(2,1)S(1)}, u32[]{:S(2)}, u32[]{:S(2)}) collective-permute-start(bf16[6,96,1,128]{3,1,2,0:T(8,128)(2,1)S(1)} %get-tuple-element.144), channel_id=1, source_target_pairs={{1,0},{2,1},{3,2},{4,3},{5,4},{6,5},{7,6},{8,7},{9,8},{10,9},{11,1... | collective-permute-start | bytes 442376 | tf_op jit(solution)/shard_map/ppermute | solution.py:17
  55.1 10.0 %collective-permute-start.4 = (bf16[6,96,1,128]{3,1,2,0:T(8,128)(2,1)S(1)}, bf16[6,96,1,128]{3,1,2,0:T(8,128)(2,1)S(1)}, u32[]{:S(2)}, u32[]{:S(2)}) collective-permute-start(bf16[6,96,1,128]{3,1,2,0:T(8,128)(2,1)S(1)} %get-tuple-element.143), channel_id=1, source_target_pairs={{0,1},{1,2},{2,3},{3,4},{4,5},{5,6},{6,7},{7,8},{8,9},{9,10},{10,1... | collective-permute-start | bytes 442376 | tf_op jit(solution)/shard_map/ppermute | solution.py:16
  72.7 15.0 %collective-permute-start.7 = (bf16[8,96,1,128]{3,1,2,0:T(8,128)(2,1)S(1)}, bf16[8,96,1,128]{3,1,2,0:T(8,128)(2,1)S(1)}, u32[]{:S(2)}, u32[]{:S(2)}) collective-permute-start(bf16[8,96,1,128]{3,1,2,0:T(8,128)(2,1)S(1)} %get-tuple-element.130), channel_id=1, source_target_pairs={{1,0},{2,1},{3,2},{4,3},{5,4},{6,5},{7,6},{8,7},{9,8},{10,9},{11,1... | collective-permute-start | bytes 589832 | tf_op jit(solution)/shard_map/ppermute | solution.py:17
  74.6 13.1 %collective-permute-start.6 = (bf16[8,96,1,128]{3,1,2,0:T(8,128)(2,1)S(1)}, bf16[8,96,1,128]{3,1,2,0:T(8,128)(2,1)S(1)}, u32[]{:S(2)}, u32[]{:S(2)}) collective-permute-start(bf16[8,96,1,128]{3,1,2,0:T(8,128)(2,1)S(1)} %get-tuple-element.129), channel_id=1, source_target_pairs={{0,1},{1,2},{2,3},{3,4},{4,5},{5,6},{6,7},{7,8},{8,9},{9,10},{10,1... | collective-permute-start | bytes 589832 | tf_op jit(solution)/shard_map/ppermute | solution.py:16
  94.5 2.3 copy-start.3
  94.5 4.1 copy-start.4
  104.3 768.2 %copy-start.1 = (bf16[6,4,4,128]{3,2,1,0:T(4,128)(2,1)S(1)}, bf16[6,4,4,128]{3,2,1,0:T(4,128)(2,1)}, u32[]{:S(2)}) copy-start(bf16[6,4,4,128]{3,2,1,0:T(4,128)(2,1)} %param.30) | copy-start | bytes 73732
Sparse Core Ops, SparseCore 0:
  86.1 783.4 all-reduce.7
where the time goes:
time: 880 us; the launch traced here: 879 us
  blocking collectives  396 us (45%)
  waiting for transfers between devices  371 us (42%)
  starting transfers between devices  36.7 us (4%)
  matrix products  24.9 us (3%)
  local copies, waits for them, and re-layouts  22.5 us (3%)
  between operations  14.8 us (2%)
  other arithmetic  14.1 us (2%)
    psum x1, blocking collectives, local(): main_sum, head_sum = lax.psum((main_part, head_part), 'slab')  396 us
    psum x1, waiting for transfers between devices, local(): main_sum, head_sum = lax.psum((main_part, head_part), 'slab')  365 us
    ppermute x4, starting transfers between devices, padded_2(): before = lax.ppermute(last, axis, up)  25.7 us
  transfers between devices with their start and end apart: 9, of which 3 were waited for; matrix products, arithmetic and copies ran while one was open for 3% of the time, Pallas kernels for 0%

commit v1 on v0

v1 whole, which is shorter than its diff:
```python
import functools

import jax
import jax.numpy as jnp
from jax import lax
from jax.experimental import pallas as pl
from jax.experimental.pallas import tpu as pltpu
from jax.sharding import PartitionSpec as P

EPS = 1e-06
MESH = pl.DeviceIdType.MESH
F32 = jnp.float32
BF16 = jnp.bfloat16
C = 96
FR = 6
COLS = 128
K3 = 9 * C
TILES = 128


def dot(a, b):
    return lax.dot_general(a, b, (((1,), (0,)), ((), ())), preferred_element_type=F32)


def dot_nt(a, b):
    return lax.dot_general(a, b, (((1,), (1,)), ((), ())), preferred_element_type=F32)


def lane_of(value):
    return lax.broadcasted_iota(jnp.int32, value.shape, 1)


def later(value):
    return jnp.where(lane_of(value) == 0, 0.0, pltpu.roll(value, 1, 1))


def earlier(value):
    return jnp.where(lane_of(value) == COLS - 1, 0.0, pltpu.roll(value, COLS - 1, 1))


def by_row(shift, value):
    parts = [shift(value[:, i : i + COLS]) for i in range(0, value.shape[1], COLS)]
    return jnp.concatenate(parts, axis=1)


def wide(gain, width):
    return jnp.concatenate([gain] * (width // COLS), axis=1)


def norm_parts(value, gain):
    meansq = jnp.sum(value * value, axis=0, keepdims=True) * (1.0 / C)
    root = lax.rsqrt(meansq + EPS)
    unit = value * root
    normed = unit * gain
    sig = 0.5 * jnp.tanh(0.5 * normed) + 0.5
    return root, unit, normed, sig


def norm_pull(parts, gain, cot):
    root, unit, normed, sig = parts
    inner = cot * gain * (sig * (1.0 + normed * (1.0 - sig)))
    mean = jnp.sum(inner * unit, axis=0, keepdims=True) * (1.0 / C)
    return root * (inner - unit * mean)


def kernel(
    slabs,
    x_ref,
    mc_ref,
    hc_ref,
    gin_ref,
    gout_ref,
    mw_ref,
    hw_ref,
    ag_ref,
    tab_ref,
    idx_ref,
    ord_ref,
    gi_ref,
    gm_ref,
    gh_ref,
    stage,
    xs,
    gains,
    hin,
    hin_t,
    hin_b,
    head,
    wtmp,
    wf,
    wt,
    hwt,
    pg_own,
    pg_send,
    pg_halo,
    taps,
    dout,
    dob,
    dob_t,
    dob_b,
    dsh,
    grads,
    piece,
    got1,
    sum1,
    got2,
    half3,
    got3,
    full,
    hs,
    hr,
    ps,
    pr,
    ds,
    dr,
    s1,
    r1,
    s2,
    r2,
    s3,
    r3,
    s4,
    r4,
    s5,
    r5,
):
    planes = slabs // 4
    me = lax.axis_index("slab")
    core = me % 2
    place = me % 4
    zh = place // 2
    xy = me // 4
    up = (me + slabs - 1) % slabs
    down = (me + 1) % slabs
    sibling = me + 1 - 2 * core
    zpartner = me + 2 - 4 * zh

    def in_plane(k):
        return ((xy + k) % planes) * 4 + place

    def remote(src, dst, send, recv, to):
        return pltpu.make_async_remote_copy(
            src_ref=src,
            dst_ref=dst,
            send_sem=send,
            recv_sem=recv,
            device_id={"slab": to},
            device_id_type=MESH,
        )

    barrier = pltpu.get_barrier_semaphore()

    def greet(to):
        pl.semaphore_signal(barrier, inc=1, device_id={"slab": to}, device_id_type=MESH)

    greet(up)
    greet(down)
    greet(zpartner)
    for k in range(1, planes):
        greet(in_plane(k))

    def split_rows(f, source):
        stage[f] = source.astype(F32)
        return jnp.concatenate(
            [stage[f, pl.ds(r, C, stride=4), :] for r in range(4)], axis=1
        )

    for j in range(2):
        hin[j] = split_rows(j, mc_ref[j]).astype(BF16)
        head[j] = split_rows(j, hc_ref[j]).astype(BF16)

    pg_own[...] = jnp.zeros_like(pg_own)
    for f in range(FR):
        picked = []
        for a in range(4):
            total = None
            for j in range(FR):
                weight = jnp.where(ord_ref[j] == f, 1.0, 0.0).astype(F32)
                term = ag_ref[j, a].astype(F32) * weight
                total = term if total is None else total + term
            picked.append(total)
        row = idx_ref[f]
        for c in range(3):
            value = picked[0] * tab_ref[row, c, 0]
            for a in range(1, 4):
                value = value + picked[a] * tab_ref[row, c, a]
            for r in range(4):
                pg_own[r, 6 + 3 * f + c : 7 + 3 * f + c, :] = value[r : r + 1, :]
    pg_send[...] = pg_own[...].astype(BF16)

    pl.semaphore_wait(barrier, planes + 2)

    def pg_copy(side):
        return remote(
            pg_send.at[0 if side == 0 else 3],
            pg_halo.at[1 - side],
            ps.at[side],
            pr.at[1 - side],
            up if side == 0 else down,
        )

    for side in range(2):
        pg_copy(side).start()

    def hin_copy(side, f):
        if side == 0:
            return remote(hin.at[f, :, pl.ds(0, COLS)], hin_b.at[f], hs.at[0, f], hr.at[1, f], up)
        return remote(hin.at[f, :, pl.ds(3 * COLS, COLS)], hin_t.at[f], hs.at[1, f], hr.at[0, f], down)

    def dob_copy(side, f):
        if side == 0:
            return remote(dob.at[f, :, pl.ds(0, COLS)], dob_b.at[f], ds.at[0, f], dr.at[1, f], up)
        return remote(dob.at[f, :, pl.ds(3 * COLS, COLS)], dob_t.at[f], ds.at[1, f], dr.at[0, f], down)

    for j in range(2):
        for side in range(2):
            hin_copy(side, j).start()

    gains[0] = jnp.broadcast_to(gin_ref[...], (COLS, C)).T
    gains[1] = jnp.broadcast_to(gout_ref[...], (COLS, C)).T

    def make_h(f, carry):
        value = split_rows(f, x_ref[f])
        xs[f] = value
        _, _, normed, sig = norm_parts(value, wide(gains[0], 4 * COLS))
        hin[f + 2] = (normed * sig).astype(BF16)
        for side in range(2):
            hin_copy(side, f + 2).start()
        return carry

    lax.fori_loop(0, FR, make_h, 0)

    for x in range(3):
        for y in range(3):
            for t in range(3):
                at = (y * 3 + t) * C
                wtmp[0, x * C : (x + 1) * C, at : at + C] = mw_ref[t, y, x].astype(F32)
                wtmp[1, x * C : (x + 1) * C, at : at + C] = mw_ref[2 - t, 2 - y, x].astype(F32).T
    wf[...] = wtmp[0, :, 0:K3].astype(BF16)
    wt[...] = wtmp[1, :, 0:K3].astype(BF16)
    grads[0:C, 0:C] = jnp.zeros((C, C), F32)
    for y in range(3):
        for x in range(3):
            for t in range(3):
                at = y * 32 + x * 9 + t * 3
                grads[at : at + 3, 0:C] = hw_ref[2 - t, y, x].astype(F32)
    hwt[...] = grads[0:C, 0:C].T.astype(BF16)

    for side in range(2):
        pg_copy(side).wait_recv()

    @pl.when(me == 0)
    def _():
        pg_halo[0] = jnp.zeros((32, COLS), BF16)

    @pl.when(me == slabs - 1)
    def _():
        pg_halo[1] = jnp.zeros((32, COLS), BF16)

    rows6 = [pg_halo[0]] + [pg_send[r] for r in range(4)] + [pg_halo[1]]
    rows6 = [value.astype(F32) for value in rows6]
    stack = jnp.concatenate(
        [
            jnp.concatenate([earlier(value) for value in rows6], axis=1),
            jnp.concatenate(rows6, axis=1),
            jnp.concatenate([later(value) for value in rows6], axis=1),
        ],
        axis=0,
    ).astype(BF16)
    out_row = lax.broadcasted_iota(jnp.int32, (8 * 32, C), 0)
    in_row = lax.broadcasted_iota(jnp.int32, (8 * 32, C), 1)
    frame = lax.shift_right_logical(out_row, 5)
    tap = out_row - 32 * frame
    col = jnp.where(tap >= 9, 1, 0) + jnp.where(tap >= 18, 1, 0)
    source = col * 32 + frame * 3 + (tap - 9 * col)
    chosen = jnp.where((in_row == source) & (tap < 27), 1.0, 0.0).astype(BF16)
    spread = dot(chosen, stack).astype(BF16)
    for f in range(8):
        taps[f] = spread[f * 32 : (f + 1) * 32, :]

    def pixel_taps(f, first, rows):
        return jnp.concatenate(
            [taps[f, :, pl.ds((2 - y + first) * COLS, rows * COLS)] for y in range(3)], axis=0
        )

    def finish_out(f, cells, image, conv, cot):
        gain = wide(gains[1], 2 * COLS)
        out = image + conv
        parts = norm_parts(out, gain)
        hh = (parts[2] * parts[3]).astype(BF16)
        grad = norm_pull(parts, gain, cot)
        before = by_row(earlier, grad).astype(BF16)
        after = by_row(later, grad).astype(BF16)
        here = grad.astype(BF16)
        for n, at in enumerate(cells):
            part = slice(n * COLS, (n + 1) * COLS)
            lanes = slice(at * COLS, (at + 1) * COLS)
            head[f + 2, :, lanes] = hh[:, part]
            dout[f, :, lanes] = grad[:, part]
            dob[f, :, lanes] = here[:, part]
            dsh[f, 0:C, lanes] = before[:, part]
            dsh[f, C : 2 * C, lanes] = here[:, part]
            dsh[f, 2 * C : 3 * C, lanes] = after[:, part]

    def columns(z, first, last):
        return z[C : 2 * C] + by_row(first, z[0:C]) + by_row(last, z[2 * C : 3 * C])

    def middle_of(field, f):
        return jnp.concatenate(
            [field[f + t, :, y * COLS : (y + 2) * COLS] for y in range(3) for t in range(3)], axis=0
        )

    def edges_of(field, top, bottom, f):
        parts = []
        for y in range(3):
            for t in range(3):
                one = top[f + t] if y == 0 else field[f + t, :, (y - 1) * COLS : y * COLS]
                two = bottom[f + t] if y == 2 else field[f + t, :, (y + 2) * COLS : (y + 3) * COLS]
                parts.append(jnp.concatenate([one, two], axis=1))
        return jnp.concatenate(parts, axis=0)

    def forward_middle(f, carry):
        conv = columns(dot(wf[...], middle_of(hin, f)), later, earlier)
        cot = dot(hwt[...], pixel_taps(f + 2, 1, 2))
        finish_out(f, (1, 2), xs[f, :, COLS : 3 * COLS], conv, cot)
        return carry

    lax.fori_loop(0, FR, forward_middle, 0)

    def hin_arrived(f):
        for side in range(2):
            hin_copy(side, f).wait_recv()

        @pl.when(me == 0)
        def _():
            hin_t[f] = jnp.zeros((C, COLS), BF16)

        @pl.when(me == slabs - 1)
        def _():
            hin_b[f] = jnp.zeros((C, COLS), BF16)

    hin_arrived(0)
    hin_arrived(1)

    def forward_edges(f, carry):
        hin_arrived(f + 2)
        conv = columns(dot(wf[...], edges_of(hin, hin_t, hin_b, f)), later, earlier)
        window = jnp.concatenate([pixel_taps(f + 2, 0, 1), pixel_taps(f + 2, 3, 1)], axis=1)
        cot = dot(hwt[...], window)
        image = jnp.concatenate([xs[f, :, 0:COLS], xs[f, :, 3 * COLS : 4 * COLS]], axis=1)
        finish_out(f, (0, 3), image, conv, cot)
        for side in range(2):
            dob_copy(side, f).start()
        return carry

    lax.fori_loop(0, FR, forward_edges, 0)

    def main_grad(f, carry):
        parts = []
        for y in range(3):
            for t in range(3):
                if y == 0:
                    block = jnp.concatenate([hin_t[f + t], hin[f + t, :, 0 : 3 * COLS]], axis=1)
                elif y == 1:
                    block = hin[f + t]
                else:
                    block = jnp.concatenate([hin[f + t, :, COLS : 4 * COLS], hin_b[f + t]], axis=1)
                parts.append(block)
        grads[:, 0:K3] += dot_nt(dsh[f], jnp.concatenate(parts, axis=0))
        return carry

    grads[...] = jnp.zeros_like(grads)
    lax.fori_loop(0, FR, main_grad, 0)

    def head_grad(f, total):
        return total + dot_nt(pixel_taps(f, 0, 4), head[f])

    head_total = lax.fori_loop(0, 8, head_grad, jnp.zeros((C, C), F32))
    for x in range(3):
        grads[x * C : (x + 1) * C, K3 : K3 + 32] = head_total[:, 32 * x : 32 * (x + 1)]

    per = TILES // 2 // planes
    for tile in range(TILES):
        half, rest = divmod(tile, TILES // 2)
        owner, k = divmod(rest, per)
        row, lane = divmod(tile, 7)
        if row < 18:
            value = grads[row * 16 : (row + 1) * 16, lane * COLS : (lane + 1) * COLS].astype(BF16)
        else:
            value = jnp.zeros((16, COLS), BF16)
        piece[half, owner, k * 16 : (k + 1) * 16, :] = value

    def pair_copy():
        return remote(piece.at[1 - core], got1, s1, r1, sibling)

    def scatter_copy(k):
        return remote(sum1.at[(xy + k) % planes], got2.at[k], s2.at[k], r2.at[k], in_plane(k))

    def z_copy():
        return remote(half3, got3, s3, r3, zpartner)

    def gather_copy(k):
        return remote(full.at[core, xy], full.at[core, xy], s4.at[k], r4.at[k], in_plane(k))

    def forward_copy(k):
        at = (xy + planes - k) % planes
        return remote(full.at[core, at], full.at[core, at], s5.at[k], r5.at[k], sibling)

    pair_copy().start()

    dob[6] = jnp.zeros((C, 4 * COLS), BF16)
    dob[7] = jnp.zeros((C, 4 * COLS), BF16)
    for f in (6, 7):
        dob_t[f] = jnp.zeros((C, COLS), BF16)
        dob_b[f] = jnp.zeros((C, COLS), BF16)

    def finish_in(f, cells, conv):
        gain = wide(gains[0], 2 * COLS)
        lanes = [slice(at * COLS, (at + 1) * COLS) for at in cells]
        image = jnp.concatenate([xs[f, :, at] for at in lanes], axis=1)
        grad = norm_pull(norm_parts(image, gain), gain, conv)
        for n, at in enumerate(cells):
            value = grad[:, n * COLS : (n + 1) * COLS] + dout[f, :, lanes[n]]
            gi_ref[f, pl.ds(at, C, stride=4), :] = value

    def backward_middle(f, carry):
        finish_in(f, (1, 2), columns(dot(wt[...], middle_of(dob, f)), earlier, later))
        return carry

    def backward_edges(f, carry):
        window = edges_of(dob, dob_t, dob_b, f)
        finish_in(f, (0, 3), columns(dot(wt[...], window), earlier, later))
        return carry

    lax.fori_loop(0, 2, backward_middle, 0)

    pair_copy().wait_recv()
    sum1[...] = (piece[core].astype(F32) + got1[...].astype(F32)).astype(BF16)

    def start_scatter(k, carry):
        scatter_copy(k).start()
        return carry

    lax.fori_loop(1, planes, start_scatter, 0)
    lax.fori_loop(2, FR, backward_middle, 0)

    def add_piece(k, total):
        scatter_copy(k).wait_recv()
        return total + got2[k].astype(F32)

    mine = lax.fori_loop(1, planes, add_piece, sum1[xy].astype(F32))
    half3[...] = mine.astype(BF16)
    z_copy().start()

    for f in range(FR):
        for side in range(2):
            dob_copy(side, f).wait_recv()

    @pl.when(me == 0)
    def _():
        dob_t[0:FR] = jnp.zeros((FR, C, COLS), BF16)

    @pl.when(me == slabs - 1)
    def _():
        dob_b[0:FR] = jnp.zeros((FR, C, COLS), BF16)

    lax.fori_loop(0, 2, backward_edges, 0)

    z_copy().wait_recv()
    full[core, xy] = (half3[...].astype(F32) + got3[...].astype(F32)).astype(BF16)

    def start_gather(k, carry):
        gather_copy(k).start()
        return carry

    forward_copy(0).start()
    lax.fori_loop(1, planes, start_gather, 0)
    lax.fori_loop(2, FR, backward_edges, 0)

    def pass_on(k, carry):
        gather_copy(k).wait_recv()
        forward_copy(k).start()
        return carry

    lax.fori_loop(1, planes, pass_on, 0)

    def passed_on(k, carry):
        forward_copy(k).wait_recv()
        return carry

    lax.fori_loop(0, planes, passed_on, 0)

    scale = (1.0 / (FR * slabs * 4 * COLS)) ** 0.5
    for tile in range(18 * 7):
        half, rest = divmod(tile, TILES // 2)
        owner, k = divmod(rest, per)
        row, lane = divmod(tile, 7)
        value = full[half, owner, k * 16 : (k + 1) * 16, :].astype(F32) * scale
        grads[row * 16 : (row + 1) * 16, lane * COLS : (lane + 1) * COLS] = value
    for x in range(3):
        for y in range(3):
            for t in range(3):
                at = (y * 3 + t) * C
                gm_ref[t, y, x] = grads[x * C : (x + 1) * C, at : at + C]
    head_total = jnp.concatenate(
        [grads[x * C : (x + 1) * C, K3 : K3 + 32] for x in range(3)], axis=1
    )
    for y in range(3):
        for x in range(3):
            for t in range(3):
                at = y * 32 + x * 9 + t * 3
                gh_ref[2 - t, y, x] = head_total[at : at + 3, :]

    for side in range(2):
        pg_copy(side).wait_send()

    def hin_left(f, carry):
        for side in range(2):
            hin_copy(side, f).wait_send()
        return carry

    lax.fori_loop(0, 8, hin_left, 0)

    def dob_left(f, carry):
        for side in range(2):
            dob_copy(side, f).wait_send()
        return carry

    lax.fori_loop(0, FR, dob_left, 0)
    pair_copy().wait_send()
    z_copy().wait_send()
    forward_copy(0).wait_send()

    def sums_left(k, carry):
        scatter_copy(k).wait_send()
        gather_copy(k).wait_send()
        forward_copy(k).wait_send()
        return carry

    lax.fori_loop(1, planes, sums_left, 0)


def local(slabs, *operands):
    (x, mc, hc, gin, gout, mw, hw, ag, tab, idx, order) = operands
    planes = slabs // 4
    piece = (planes, 1024 // planes, COLS)
    vmem = pl.BlockSpec(memory_space=pltpu.VMEM)
    smem = pl.BlockSpec(memory_space=pltpu.SMEM)
    dma = pltpu.SemaphoreType.DMA
    gi, gm, gh = pl.pallas_call(
        functools.partial(kernel, slabs),
        out_shape=(
            jax.ShapeDtypeStruct((FR, 4 * C, COLS), F32),
            jax.ShapeDtypeStruct((3, 3, 3, C, C), F32),
            jax.ShapeDtypeStruct((3, 3, 3, 3, C), F32),
        ),
        in_specs=[vmem] * 8 + [smem] * 3,
        out_specs=[vmem] * 3,
        scratch_shapes=[
            pltpu.VMEM((FR, 4 * C, COLS), F32),
            pltpu.VMEM((FR, C, 4 * COLS), F32),
            pltpu.VMEM((2, C, COLS), F32),
            pltpu.VMEM((8, C, 4 * COLS), BF16),
            pltpu.VMEM((8, C, COLS), BF16),
            pltpu.VMEM((8, C, COLS), BF16),
            pltpu.VMEM((8, C, 4 * COLS), BF16),
            pltpu.VMEM((2, 3 * C, 7 * COLS), F32),
            pltpu.VMEM((3 * C, K3), BF16),
            pltpu.VMEM((3 * C, K3), BF16),
            pltpu.VMEM((C, C), BF16),
            pltpu.VMEM((4, 32, COLS), F32),
            pltpu.VMEM((4, 32, COLS), BF16),
            pltpu.VMEM((2, 32, COLS), BF16),
            pltpu.VMEM((8, 32, 6 * COLS), BF16),
            pltpu.VMEM((FR, C, 4 * COLS), F32),
            pltpu.VMEM((8, C, 4 * COLS), BF16),
            pltpu.VMEM((8, C, COLS), BF16),
            pltpu.VMEM((8, C, COLS), BF16),
            pltpu.VMEM((FR, 3 * C, 4 * COLS), BF16),
            pltpu.VMEM((3 * C, 7 * COLS), F32),
            pltpu.VMEM((2,) + piece, BF16),
            pltpu.VMEM(piece, BF16),
            pltpu.VMEM(piece, BF16),
            pltpu.VMEM(piece, BF16),
            pltpu.VMEM(piece[1:], BF16),
            pltpu.VMEM(piece[1:], BF16),
            pltpu.VMEM((2,) + piece, BF16),
            dma((2, 8)),
            dma((2, 8)),
            dma((2,)),
            dma((2,)),
            dma((2, FR)),
            dma((2, FR)),
            dma,
            dma,
            dma((planes,)),
            dma((planes,)),
            dma,
            dma,
            dma((planes,)),
            dma((planes,)),
            dma((planes,)),
            dma((planes,)),
        ],
        compiler_params=pltpu.CompilerParams(
            collective_id=0, has_side_effects=True, vmem_limit_bytes=56 * 2**20
        ),
    )(
        x.reshape(FR, 4 * C, COLS),
        mc.reshape(2, 4 * C, COLS),
        hc.reshape(2, 4 * C, COLS),
        gin.reshape(1, C),
        gout.reshape(1, C),
        mw,
        hw,
        ag,
        tab,
        idx,
        order,
    )
    return gi.reshape(FR, C, 4, COLS), gm, gh


def solution(mesh):
    tile = P("video", None, "slab", None)
    whole = P("video", None, None, None, None)
    placed = (tile, tile, tile, P(), P(), P(), P(), tile, P(), P("video"), P())
    return jax.shard_map(
        functools.partial(local, mesh.shape["slab"]),
        mesh=mesh,
        in_specs=placed,
        out_specs=(tile, whole, whole),
        check_vma=False,
    )
```

time: 880 us -> 60.4 us (0.07)
  blocking collectives: 396 us -> 0 us
  waiting for transfers between devices: 371 us -> 0 us
  Pallas kernels: 0 us -> 54 us
  starting transfers between devices: 36.7 us -> 0 us
  matrix products: 24.9 us -> 0 us
  local copies, waits for them, and re-layouts: 22.5 us -> 5.55 us
  between operations: 14.8 us -> 0.65 us
  other arithmetic: 14.1 us -> 0 us
    psum x1 -> x0, blocking collectives: 396 us -> none  [local(): main_sum, head_sum = lax.psum((main_part, head_part), 'slab')]
    psum x1 -> x0, waiting for transfers between devices: 365 us -> none  [local(): main_sum, head_sum = lax.psum((main_part, head_part), 'slab')]
    pallas_call x0 -> x1, Pallas kernels: none -> 54 us  [local(): pl.pallas_call(functools.partial(kernel, slabs), out_shape=(jax.ShapeDtyp...]
    ppermute x8 -> x0, starting transfers between devices: 36.6 us -> none  [the longest x4 25.7 us: padded_2(): before = lax.ppermute(last, axis, up)]
    dot_general x18 -> x0, matrix products: 24.9 us -> none  [the longest x6 13.9 us: weight_grad(): jnp.einsum('fohw,fkhw->ok', grad, stack, preferred_element_type=jnp.float32)]
    unnamed x47 -> x8, local copies, waits for them, and re-layouts: 16.7 us -> 5.55 us
  transfers between devices with their start and end apart: 9 -> 0, of which waited for: 3 -> 0; matrix products, arithmetic and copies ran while one was open for 3% -> 0% of each run, Pallas kernels for 0% -> 0%
where the time goes in v1:
time: 60.4 us; the launch traced here: 60.2 us
  Pallas kernels  54 us (89%)
  local copies, waits for them, and re-layouts  5.55 us (9%)
  between operations  0.65 us (1%)
    pallas_call x1, Pallas kernels, local(): pl.pallas_call(functools.partial(kernel, slabs), out_shape=(jax.ShapeDtyp...  54 us
    unnamed x8, local copies, waits for them, and re-layouts  5.55 us

profile of v1, /device:TPU:1, one launch (start us, length us, event | category | flops | bytes accessed | tf_op | source)
XLA Modules:
  0.0 60.2 jit_solution(13005305496683247731)
XLA Ops:
  0.6 1.4 %copy.14.tab_ref = f32[16,3,4]{2,1,0:T(4,128)} copy(f32[16,3,4]{0,2,1:T(4,128)} %param.19) | data formatting | bytes 1536 | tf_op args[8]
  2.0 54.0 %shard_map.130 = (f32[6,384,128]{2,1,0:T(8,128)}, f32[3,3,3,96,96]{4,3,2,1,0:T(8,128)}, f32[3,3,3,3,96]{4,3,2,1,0:T(4,128)}) custom-call(bf16[6,384,128]{2,1,0:T(8,128)(2,1)} %bitcast.7, bf16[2,384,128]{2,1,0:T(8,128)(2,1)} %bitcast.8, bf16[2,384,128]{2,1,0:T(8,128)(2,1)} %bitcast.9, f32[1,96]{1,0:T(1,128)} %bitcast.10, f32[1,96]{1,0:T(1,128)} %bitcast.11, ...), custom_call_target="tpu_custom_call" | custom-call | tf_op jit(solution)/shard_map/pallas_call | solution.py:550
  56.0 0.0 copy-start
  56.0 2.5 %copy.18 = f32[6,96,4,128]{3,2,1,0:T(4,128)} copy(f32[6,96,4,128]{3,2,1,0:T(4,128)} %bitcast.6) | data formatting | bytes 2359296
  58.5 0.0 copy-done
  58.5 0.0 copy-start.1
  58.5 1.1 %copy.19 = f32[3,3,3,96,96]{4,3,2,1,0:T(8,128)} copy(f32[3,3,3,96,96]{4,3,2,1,0:T(8,128)S(1)} %copy-done) | data formatting | bytes 1990656
  59.6 0.0 copy-done.1
  59.6 0.6 %copy.20 = f32[3,3,3,3,96]{4,3,2,1,0:T(4,128)} copy(f32[3,3,3,3,96]{4,3,2,1,0:T(4,128)S(1)} %copy-done.1) | data formatting | bytes 62208
Async XLA Ops:
  56.0 2.5 %copy-start = (f32[3,3,3,96,96]{4,3,2,1,0:T(8,128)S(1)}, f32[3,3,3,96,96]{4,3,2,1,0:T(8,128)}, u32[]{:S(2)}) copy-start(f32[3,3,3,96,96]{4,3,2,1,0:T(8,128)} %get-tuple-element.13) | copy-start | bytes 2985988
  58.5 1.1 %copy-start.1 = (f32[3,3,3,3,96]{4,3,2,1,0:T(4,128)S(1)}, f32[3,3,3,3,96]{4,3,2,1,0:T(4,128)}, u32[]{:S(2)}) copy-start(f32[3,3,3,3,96]{4,3,2,1,0:T(4,128)} %get-tuple-element.14) | copy-start | bytes 93316

commit v2 on v1

v2 whole, which is shorter than its diff:
```python
import functools

import jax
import jax.numpy as jnp
from jax import lax
from jax.experimental import pallas as pl
from jax.experimental.pallas import tpu as pltpu
from jax.sharding import PartitionSpec as P

EPS = 1e-06
MESH = pl.DeviceIdType.MESH
F32 = jnp.float32
BF16 = jnp.bfloat16
C = 96
FR = 6
COLS = 128
K3 = 9 * C


def dot(a, b):
    return lax.dot_general(a, b, (((1,), (0,)), ((), ())), preferred_element_type=F32)


def dot_nt(a, b):
    return lax.dot_general(a, b, (((1,), (1,)), ((), ())), preferred_element_type=F32)


def lane_of(value):
    return lax.broadcasted_iota(jnp.int32, value.shape, 1)


def later(value):
    return jnp.where(lane_of(value) == 0, 0.0, pltpu.roll(value, 1, 1))


def earlier(value):
    return jnp.where(lane_of(value) == COLS - 1, 0.0, pltpu.roll(value, COLS - 1, 1))


def by_row(shift, value):
    parts = [shift(value[:, i : i + COLS]) for i in range(0, value.shape[1], COLS)]
    return jnp.concatenate(parts, axis=1)


def wide(gain, width):
    return jnp.concatenate([gain] * (width // COLS), axis=1)


def norm_parts(value, gain):
    meansq = jnp.sum(value * value, axis=0, keepdims=True) * (1.0 / C)
    root = lax.rsqrt(meansq + EPS)
    unit = value * root
    normed = unit * gain
    sig = 0.5 * jnp.tanh(0.5 * normed) + 0.5
    return root, unit, normed, sig


def norm_pull(parts, gain, cot):
    root, unit, normed, sig = parts
    inner = cot * gain * (sig * (1.0 + normed * (1.0 - sig)))
    mean = jnp.sum(inner * unit, axis=0, keepdims=True) * (1.0 / C)
    return root * (inner - unit * mean)


def kernel(
    slabs,
    x_hbm,
    mc_hbm,
    hc_hbm,
    gin_hbm,
    gout_hbm,
    mw_hbm,
    hw_hbm,
    ag_hbm,
    tab_hbm,
    idx_hbm,
    ord_hbm,
    gi_hbm,
    sums_hbm,
    x_ref,
    mc_ref,
    hc_ref,
    gin_ref,
    gout_ref,
    mw_ref,
    hw_ref,
    ag_ref,
    tab_ref,
    idx_ref,
    ord_ref,
    gi_ref,
    stage,
    xs,
    gains,
    hin,
    hin_t,
    hin_b,
    head,
    wtmp,
    wf,
    wt,
    hwt,
    pg_own,
    pg_send,
    pg_halo,
    taps,
    dout,
    dob,
    dob_t,
    dob_b,
    dsh_mid,
    dsh_edge,
    mid_grads,
    head_mid,
    head_sum,
    grads,
    piece,
    got1,
    sum1,
    got2,
    half3,
    got3,
    full,
    ins,
    outs,
    hs,
    hr,
    ps,
    pr,
    ds,
    dr,
    s1,
    r1,
    s2,
    r2,
    s3,
    r3,
    s4,
    r4,
    s5,
    r5,
):
    me = lax.axis_index("slab")
    core = me % 2
    place = me % 4
    zh = place // 2
    xy = me // 4
    planes = slabs // 4
    up = (me + slabs - 1) % slabs
    down = (me + 1) % slabs
    sibling = me + 1 - 2 * core
    zpartner = me + 2 - 4 * zh

    def in_plane(k):
        return ((xy + k) % planes) * 4 + place

    pairs = (
        (x_hbm, x_ref),
        (mc_hbm, mc_ref),
        (hc_hbm, hc_ref),
        (gin_hbm, gin_ref),
        (gout_hbm, gout_ref),
        (mw_hbm, mw_ref),
        (hw_hbm, hw_ref),
        (ag_hbm, ag_ref),
        (tab_hbm, tab_ref),
        (idx_hbm, idx_ref),
        (ord_hbm, ord_ref),
    )
    loads = [pltpu.make_async_copy(a, b, ins.at[n]) for n, (a, b) in enumerate(pairs)]

    def remote(src, dst, send, recv, to):
        return pltpu.make_async_remote_copy(
            src_ref=src,
            dst_ref=dst,
            send_sem=send,
            recv_sem=recv,
            device_id={"slab": to},
            device_id_type=MESH,
        )

    barrier = pltpu.get_barrier_semaphore()

    def greet(to):
        pl.semaphore_signal(barrier, inc=1, device_id={"slab": to}, device_id_type=MESH)

    greet(up)
    greet(down)
    greet(zpartner)
    for k in range(1, planes):
        greet(in_plane(k))
    for n in (1, 0, 3, 8, 9, 10, 7, 2, 5, 6, 4):
        loads[n].start()

    def split_rows(f, source):
        stage[f] = source.astype(F32)
        return jnp.concatenate(
            [stage[f, pl.ds(r, C, stride=4), :] for r in range(4)], axis=1
        )

    loads[1].wait()
    for j in range(2):
        hin[j] = split_rows(j, mc_ref[j]).astype(BF16)

    def pg_copy(side):
        return remote(
            pg_send.at[0 if side == 0 else 3],
            pg_halo.at[1 - side],
            ps.at[side],
            pr.at[1 - side],
            up if side == 0 else down,
        )

    def hin_copy(side, f):
        if side == 0:
            return remote(hin.at[f, :, pl.ds(0, COLS)], hin_b.at[f], hs.at[0, f], hr.at[1, f], up)
        return remote(hin.at[f, :, pl.ds(3 * COLS, COLS)], hin_t.at[f], hs.at[1, f], hr.at[0, f], down)

    def dob_copy(side, f):
        if side == 0:
            return remote(dob.at[f, :, pl.ds(0, COLS)], dob_b.at[f], ds.at[0, f], dr.at[1, f], up)
        return remote(dob.at[f, :, pl.ds(3 * COLS, COLS)], dob_t.at[f], ds.at[1, f], dr.at[0, f], down)

    for n in (7, 8, 9, 10):
        loads[n].wait()
    pg_own[...] = jnp.zeros_like(pg_own)
    for f in range(FR):
        picked = []
        for a in range(4):
            total = None
            for j in range(FR):
                weight = jnp.where(ord_ref[j] == f, 1.0, 0.0).astype(F32)
                term = ag_ref[j, a].astype(F32) * weight
                total = term if total is None else total + term
            picked.append(total)
        row = idx_ref[f]
        for c in range(3):
            value = picked[0] * tab_ref[c, 0, row]
            for a in range(1, 4):
                value = value + picked[a] * tab_ref[c, a, row]
            for r in range(4):
                pg_own[r, 6 + 3 * f + c : 7 + 3 * f + c, :] = value[r : r + 1, :]
    pg_send[...] = pg_own[...].astype(BF16)
    loads[0].wait()
    loads[3].wait()
    gains[0] = jnp.broadcast_to(gin_ref[...], (COLS, C)).T
    pl.semaphore_wait(barrier, planes + 2)
    for side in range(2):
        pg_copy(side).start()
    for j in range(2):
        for side in range(2):
            hin_copy(side, j).start()

    def make_h(f):
        value = split_rows(f, x_ref[f])
        xs[f] = value
        _, _, normed, sig = norm_parts(value, wide(gains[0], 4 * COLS))
        hin[f + 2] = (normed * sig).astype(BF16)
        for side in range(2):
            hin_copy(side, f + 2).start()

    for f in range(0, FR):
        make_h(f)

    loads[4].wait()
    gains[1] = jnp.broadcast_to(gout_ref[...], (COLS, C)).T

    loads[5].wait()
    for x in range(3):
        for y in range(3):
            for t in range(3):
                at = (y * 3 + t) * C
                wtmp[0, x * C : (x + 1) * C, at : at + C] = mw_ref[t, y, x].astype(F32)
                wtmp[1, x * C : (x + 1) * C, at : at + C] = mw_ref[2 - t, 2 - y, x].astype(F32).T
    wf[...] = wtmp[0, :, 0:K3].astype(BF16)
    wt[...] = wtmp[1, :, 0:K3].astype(BF16)
    loads[6].wait()
    grads[0:C, 0:C] = jnp.zeros((C, C), F32)
    for y in range(3):
        for x in range(3):
            for t in range(3):
                at = y * 32 + x * 9 + t * 3
                grads[at : at + 3, 0:C] = hw_ref[2 - t, y, x].astype(F32)
    hwt[...] = grads[0:C, 0:C].T.astype(BF16)
    loads[2].wait()
    for j in range(2):
        head[j] = split_rows(j, hc_ref[j]).astype(BF16)

    out_row = lax.broadcasted_iota(jnp.int32, (8 * 32, C), 0)
    in_row = lax.broadcasted_iota(jnp.int32, (8 * 32, C), 1)
    frame = lax.shift_right_logical(out_row, 5)
    tap = out_row - 32 * frame
    col = jnp.where(tap >= 9, 1, 0) + jnp.where(tap >= 18, 1, 0)
    source = col * 32 + frame * 3 + (tap - 9 * col)
    chosen = jnp.where((in_row == source) & (tap < 27), 1.0, 0.0).astype(BF16)

    def spread(rows, lanes):
        rows = [value.astype(F32) for value in rows]
        stack = jnp.concatenate(
            [
                jnp.concatenate([earlier(value) for value in rows], axis=1),
                jnp.concatenate(rows, axis=1),
                jnp.concatenate([later(value) for value in rows], axis=1),
            ],
            axis=0,
        )
        result = dot(chosen, stack.astype(BF16)).astype(BF16)
        for f in range(8):
            for n, at in enumerate(lanes):
                value = result[f * 32 : (f + 1) * 32, n * COLS : (n + 1) * COLS]
                taps[f, :, at * COLS : (at + 1) * COLS] = value

    spread([pg_send[r] for r in range(4)], (1, 2, 3, 4))

    def pixel_taps(f, first, rows):
        return jnp.concatenate(
            [taps[f, :, pl.ds((2 - y + first) * COLS, rows * COLS)] for y in range(3)], axis=0
        )

    def finish_out(f, cells, image, conv, cot, shifted):
        gain = wide(gains[1], 2 * COLS)
        out = image + conv
        parts = norm_parts(out, gain)
        hh = (parts[2] * parts[3]).astype(BF16)
        grad = norm_pull(parts, gain, cot)
        before = by_row(earlier, grad).astype(BF16)
        after = by_row(later, grad).astype(BF16)
        here = grad.astype(BF16)
        for n, at in enumerate(cells):
            part = slice(n * COLS, (n + 1) * COLS)
            lanes = slice(at * COLS, (at + 1) * COLS)
            head[f + 2, :, lanes] = hh[:, part]
            dout[f, :, lanes] = grad[:, part]
            dob[f, :, lanes] = here[:, part]
        shifted[0, f, 0:C] = before
        shifted[0, f, C : 3 * C // 2] = here[0 : C // 2]
        shifted[1, f, 0 : C // 2] = here[C // 2 : C]
        shifted[1, f, C // 2 : 3 * C // 2] = after

    def columns(z, first, last):
        return z[C : 2 * C] + by_row(first, z[0:C]) + by_row(last, z[2 * C : 3 * C])

    def middle_of(field, f):
        return jnp.concatenate(
            [field[f + t, :, y * COLS : (y + 2) * COLS] for y in range(3) for t in range(3)], axis=0
        )

    def edges_of(field, top, bottom, f):
        parts = []
        for y in range(3):
            for t in range(3):
                one = top[f + t] if y == 0 else field[f + t, :, (y - 1) * COLS : y * COLS]
                two = bottom[f + t] if y == 2 else field[f + t, :, (y + 2) * COLS : (y + 3) * COLS]
                parts.append(jnp.concatenate([one, two], axis=1))
        return jnp.concatenate(parts, axis=0)

    def forward_middle(f):
        conv = columns(dot(wf[...], middle_of(hin, f)), later, earlier)
        cot = dot(hwt[...], pixel_taps(f + 2, 1, 2))
        finish_out(f, (1, 2), xs[f, :, COLS : 3 * COLS], conv, cot, dsh_mid)

    for f in range(0, FR):
        forward_middle(f)

    def edge_windows(frames):
        return jnp.concatenate([edges_of(hin, hin_t, hin_b, f) for f in frames], axis=1)

    def edge_grads(half, frames):
        return jnp.concatenate([dsh_edge[half, f] for f in frames], axis=1)

    shifted = [
        jnp.concatenate([dsh_mid[half, f] for f in range(FR)], axis=1) for half in range(2)
    ]
    middle = dot_nt(
        jnp.concatenate(shifted, axis=0),
        jnp.concatenate([middle_of(hin, f) for f in range(FR)], axis=1),
    )
    mid_grads[0] = middle[0 : 3 * C // 2]
    mid_grads[1] = middle[3 * C // 2 : 3 * C]

    def head_edge_taps(f):
        return jnp.concatenate([pixel_taps(f, 0, 1), pixel_taps(f, 3, 1)], axis=1)

    def head_edges(f):
        return jnp.concatenate([head[f, :, 0:COLS], head[f, :, 3 * COLS : 4 * COLS]], axis=1)

    head_mid[...] = dot_nt(
        jnp.concatenate([pixel_taps(f, 1, 2) for f in range(8)], axis=1),
        jnp.concatenate([head[f, :, COLS : 3 * COLS] for f in range(8)], axis=1),
    )

    def hin_arrived(frames):
        for f in frames:
            for side in range(2):
                hin_copy(side, f).wait_recv()

        some = slice(frames[0], frames[-1] + 1)
        shape = (len(frames), C, COLS)

        @pl.when(me == 0)
        def _():
            hin_t[some] = jnp.zeros(shape, BF16)

        @pl.when(me == slabs - 1)
        def _():
            hin_b[some] = jnp.zeros(shape, BF16)

    for side in range(2):
        pg_copy(side).wait_recv()

    @pl.when(me == 0)
    def _():
        pg_halo[0] = jnp.zeros((32, COLS), BF16)

    @pl.when(me == slabs - 1)
    def _():
        pg_halo[1] = jnp.zeros((32, COLS), BF16)

    spread([pg_halo[0], pg_halo[1]], (0, 5))

    def forward_edges(f):
        conv = columns(dot(wf[...], edges_of(hin, hin_t, hin_b, f)), later, earlier)
        cot = dot(hwt[...], head_edge_taps(f + 2))
        image = jnp.concatenate([xs[f, :, 0:COLS], xs[f, :, 3 * COLS : 4 * COLS]], axis=1)
        finish_out(f, (0, 3), image, conv, cot, dsh_edge)

    early = range(0, 4)
    late = range(4, FR)
    hin_arrived(range(0, 6))
    for f in early:
        forward_edges(f)
    for f in early:
        for side in range(2):
            dob_copy(side, f).start()
    part = dot_nt(
        jnp.concatenate([edge_grads(0, early), edge_grads(1, early)], axis=0), edge_windows(early)
    )
    mid_grads[0] += part[0 : 3 * C // 2]
    mid_grads[1] += part[3 * C // 2 : 3 * C]
    hin_arrived(range(6, 8))
    for f in late:
        forward_edges(f)
    for f in late:
        for side in range(2):
            dob_copy(side, f).start()

    total = head_mid[...] + dot_nt(
        jnp.concatenate([head_edge_taps(f) for f in range(8)], axis=1),
        jnp.concatenate([head_edges(f) for f in range(8)], axis=1),
    )
    head_sum[0] = total[0 : C // 2]
    head_sum[1] = total[C // 2 : C]

    per = 64 // planes

    def where_is(tile):
        owner, k = divmod(tile, per)
        return owner, slice(k * 16, (k + 1) * 16)

    def tile_of(tile):
        row, lane = divmod(tile, 7)
        return grads[row * 16 : (row + 1) * 16, lane * COLS : (lane + 1) * COLS]

    def half_grads(half):
        grads[:, 0:K3] = mid_grads[half] + dot_nt(edge_grads(half, late), edge_windows(late))
        for n in range(3):
            rows = slice(n * (C // 2), (n + 1) * (C // 2))
            grads[rows, K3 : K3 + 32] = head_sum[half, :, n * 32 : (n + 1) * 32]

    def pair_copy():
        return remote(piece, got1, s1, r1, sibling)

    def scatter_copy(k):
        return remote(sum1.at[(xy + k) % planes], got2.at[k], s2.at[k], r2.at[k], in_plane(k))

    def z_copy():
        return remote(half3, got3, s3, r3, zpartner)

    def gather_copy(k):
        mine = full.at[core, xy]
        return remote(mine, mine, s4.at[k], r4.at[k], in_plane(k))

    def pass_on(k):
        one = full.at[core, (xy + planes - k) % planes]
        return remote(one, one, s5.at[k], r5.at[k], sibling)

    half_grads(1 - core)
    for tile in range(64):
        owner, rows = where_is(tile)
        value = tile_of(tile).astype(BF16) if tile < 63 else jnp.zeros((16, COLS), BF16)
        piece[owner, rows] = value
    pair_copy().start()
    half_grads(core)

    dob[6] = jnp.zeros((C, 4 * COLS), BF16)
    dob[7] = jnp.zeros((C, 4 * COLS), BF16)
    for f in (6, 7):
        dob_t[f] = jnp.zeros((C, COLS), BF16)
        dob_b[f] = jnp.zeros((C, COLS), BF16)

    def finish_in(f, cells, conv):
        gain = wide(gains[0], 2 * COLS)
        lanes = [slice(at * COLS, (at + 1) * COLS) for at in cells]
        image = jnp.concatenate([xs[f, :, at] for at in lanes], axis=1)
        grad = norm_pull(norm_parts(image, gain), gain, conv)
        for n, at in enumerate(cells):
            value = grad[:, n * COLS : (n + 1) * COLS] + dout[f, :, lanes[n]]
            gi_ref[f, pl.ds(at, C, stride=4), :] = value

    def backward_middle(f):
        finish_in(f, (1, 2), columns(dot(wt[...], middle_of(dob, f)), earlier, later))

    def backward_edges(f):
        window = edges_of(dob, dob_t, dob_b, f)
        finish_in(f, (0, 3), columns(dot(wt[...], window), earlier, later))

    pair_copy().wait_recv()
    for tile in range(64):
        owner, rows = where_is(tile)
        value = got1[owner, rows].astype(F32)
        if tile < 63:
            value = value + tile_of(tile)
        sum1[owner, rows] = value.astype(BF16)
    for k in range(1, planes):
        scatter_copy(k).start()

    for f in range(0, FR):
        backward_middle(f)

    total = sum1[xy].astype(F32)
    for k in range(1, planes):
        scatter_copy(k).wait_recv()
    for k in range(1, planes):
        total = total + got2[k].astype(F32)
    half3[...] = total.astype(BF16)
    z_copy().start()

    for f in range(FR):
        for side in range(2):
            dob_copy(side, f).wait_recv()

    @pl.when(me == 0)
    def _():
        dob_t[0:FR] = jnp.zeros((FR, C, COLS), BF16)

    @pl.when(me == slabs - 1)
    def _():
        dob_b[0:FR] = jnp.zeros((FR, C, COLS), BF16)

    for f in range(0, FR):
        backward_edges(f)
    store = pltpu.make_async_copy(gi_ref, gi_hbm, outs.at[0])
    store.start()

    z_copy().wait_recv()
    full[core, xy] = (half3[...].astype(F32) + got3[...].astype(F32)).astype(BF16)
    for k in range(1, planes):
        gather_copy(k).start()
    pass_on(0).start()
    for k in range(1, planes):
        gather_copy(k).wait_recv()
        pass_on(k).start()
    own = pltpu.make_async_copy(full.at[core], sums_hbm.at[core], outs.at[1])
    own.start()
    for k in range(planes):
        pass_on(k).wait_recv()
    other = pltpu.make_async_copy(full.at[1 - core], sums_hbm.at[1 - core], outs.at[2])
    other.start()

    for side in range(2):
        pg_copy(side).wait_send()
        for f in range(8):
            hin_copy(side, f).wait_send()
        for f in range(FR):
            dob_copy(side, f).wait_send()
    pair_copy().wait_send()
    z_copy().wait_send()
    pass_on(0).wait_send()
    for k in range(1, planes):
        scatter_copy(k).wait_send()
        gather_copy(k).wait_send()
        pass_on(k).wait_send()
    store.wait()
    own.wait()
    other.wait()


def finish(slabs, gi_hbm, sums_hbm, out_hbm, gm_hbm, gh_ref, gi, sums, grads, gm, ins, outs):
    sums_in = pltpu.make_async_copy(sums_hbm, sums, ins.at[FR])
    sums_in.start()
    gi_in = [pltpu.make_async_copy(gi_hbm.at[f], gi.at[f], ins.at[f]) for f in range(FR)]
    gi_out = [pltpu.make_async_copy(gi.at[f], out_hbm.at[f], outs.at[f]) for f in range(FR)]
    for copy in gi_in:
        copy.start()
    planes = slabs // 4
    per = 64 // planes
    scale = (1.0 / (FR * slabs * 4 * COLS)) ** 0.5
    sums_in.wait()
    for half in range(2):
        for tile in range(63):
            owner, k = divmod(tile, per)
            row, lane = divmod(tile, 7)
            at = half * (3 * C // 2) + row * 16
            value = sums[half, owner, k * 16 : (k + 1) * 16].astype(F32) * scale
            grads[at : at + 16, lane * COLS : (lane + 1) * COLS] = value
    for f in range(FR):
        gi_in[f].wait()
        gi_out[f].start()
    gm_out = []
    for t in range(3):
        for y in range(3):
            for x in range(3):
                at = (y * 3 + t) * C
                gm[t, y, x] = grads[x * C : (x + 1) * C, at : at + C]
        gm_out.append(pltpu.make_async_copy(gm.at[t], gm_hbm.at[t], outs.at[FR + t]))
        gm_out[t].start()
    head = []
    for half in range(2):
        top = half * (3 * C // 2)
        parts = [
            grads[top + n * (C // 2) : top + (n + 1) * (C // 2), K3 : K3 + 32] for n in range(3)
        ]
        head.append(jnp.concatenate(parts, axis=1))
    head = jnp.concatenate(head, axis=0)
    for y in range(3):
        for x in range(3):
            for t in range(3):
                at = y * 32 + x * 9 + t * 3
                gh_ref[2 - t, y, x] = head[at : at + 3, :]
    for copy in gi_out + gm_out:
        copy.wait()


def local(slabs, *operands):
    (x, mc, hc, gin, gout, mw, hw, ag, tab, idx, order) = operands
    planes = slabs // 4
    unit = (1024 // planes, COLS)
    plane = (planes,) + unit
    anywhere = pl.BlockSpec(memory_space=pl.ANY)
    hbm = pl.BlockSpec(memory_space=pltpu.HBM)
    vmem = pl.BlockSpec(memory_space=pltpu.VMEM)
    dma = pltpu.SemaphoreType.DMA
    operands = (
        x.reshape(FR, 4 * C, COLS),
        mc.reshape(2, 4 * C, COLS),
        hc.reshape(2, 4 * C, COLS),
        gin.reshape(1, C),
        gout.reshape(1, C),
        mw,
        hw,
        ag,
        jnp.transpose(tab, (1, 2, 0)),
        idx,
        order,
    )
    gi_shape = jax.ShapeDtypeStruct((FR, 4 * C, COLS), F32)
    gi, sums = pl.pallas_call(
        functools.partial(kernel, slabs),
        out_shape=(gi_shape, jax.ShapeDtypeStruct((2,) + plane, BF16)),
        in_specs=[anywhere] * 11,
        out_specs=[anywhere] * 2,
        scratch_shapes=[pltpu.VMEM(value.shape, value.dtype) for value in operands[:8]]
        + [pltpu.SMEM(value.shape, value.dtype) for value in operands[8:]]
        + [
            pltpu.VMEM((FR, 4 * C, COLS), F32),
            pltpu.VMEM((FR, 4 * C, COLS), F32),
            pltpu.VMEM((FR, C, 4 * COLS), F32),
            pltpu.VMEM((2, C, COLS), F32),
            pltpu.VMEM((8, C, 4 * COLS), BF16),
            pltpu.VMEM((8, C, COLS), BF16),
            pltpu.VMEM((8, C, COLS), BF16),
            pltpu.VMEM((8, C, 4 * COLS), BF16),
            pltpu.VMEM((2, 3 * C, 7 * COLS), F32),
            pltpu.VMEM((3 * C, K3), BF16),
            pltpu.VMEM((3 * C, K3), BF16),
            pltpu.VMEM((C, C), BF16),
            pltpu.VMEM((4, 32, COLS), F32),
            pltpu.VMEM((4, 32, COLS), BF16),
            pltpu.VMEM((2, 32, COLS), BF16),
            pltpu.VMEM((8, 32, 6 * COLS), BF16),
            pltpu.VMEM((FR, C, 4 * COLS), F32),
            pltpu.VMEM((8, C, 4 * COLS), BF16),
            pltpu.VMEM((8, C, COLS), BF16),
            pltpu.VMEM((8, C, COLS), BF16),
            pltpu.VMEM((2, FR, 3 * C // 2, 2 * COLS), BF16),
            pltpu.VMEM((2, FR, 3 * C // 2, 2 * COLS), BF16),
            pltpu.VMEM((2, 3 * C // 2, K3), F32),
            pltpu.VMEM((C, C), F32),
            pltpu.VMEM((2, C // 2, C), F32),
            pltpu.VMEM((3 * C // 2, 7 * COLS), F32),
            pltpu.VMEM(plane, BF16),
            pltpu.VMEM(plane, BF16),
            pltpu.VMEM(plane, BF16),
            pltpu.VMEM(plane, BF16),
            pltpu.VMEM(unit, BF16),
            pltpu.VMEM(unit, BF16),
            pltpu.VMEM((2,) + plane, BF16),
            dma((11,)),
            dma((3,)),
            dma((2, 8)),
            dma((2, 8)),
            dma((2,)),
            dma((2,)),
            dma((2, FR)),
            dma((2, FR)),
            dma,
            dma,
            dma((planes,)),
            dma((planes,)),
            dma,
            dma,
            dma((planes,)),
            dma((planes,)),
            dma((planes,)),
            dma((planes,)),
        ],
        compiler_params=pltpu.CompilerParams(
            collective_id=0, has_side_effects=True, vmem_limit_bytes=56 * 2**20
        ),
    )(*operands)
    gi, gm, gh = pl.pallas_call(
        functools.partial(finish, slabs),
        out_shape=(
            gi_shape,
            jax.ShapeDtypeStruct((3, 3, 3, C, C), F32),
            jax.ShapeDtypeStruct((3, 3, 3, 3, C), F32),
        ),
        in_specs=[hbm, hbm],
        out_specs=[hbm, hbm, vmem],
        scratch_shapes=[
            pltpu.VMEM((FR, 4 * C, COLS), F32),
            pltpu.VMEM((2,) + plane, BF16),
            pltpu.VMEM((3 * C, 7 * COLS), F32),
            pltpu.VMEM((3, 3, 3, C, C), F32),
            dma((FR + 1,)),
            dma((FR + 3,)),
        ],
        compiler_params=pltpu.CompilerParams(vmem_limit_bytes=60 * 2**20),
    )(gi, sums)
    return gi.reshape(FR, C, 4, COLS), gm, gh


def solution(mesh):
    tile = P("video", None, "slab", None)
    whole = P("video", None, None, None, None)
    placed = (tile, tile, tile, P(), P(), P(), P(), tile, P(), P("video"), P())
    return jax.shard_map(
        functools.partial(local, mesh.shape["slab"]),
        mesh=mesh,
        in_specs=placed,
        out_specs=(tile, whole, whole),
        check_vma=False,
    )
```

time: 60.4 us -> 49.9 us (0.83)
  local copies, waits for them, and re-layouts: 5.55 us -> 0 us
  Pallas kernels: 54 us -> 48.5 us
    unnamed x8 -> x0, local copies, waits for them, and re-layouts: 5.55 us -> none
    pallas_call x1 -> x2, Pallas kernels: 54 us -> 48.5 us  [the longest x1 45.1 us: local(): pl.pallas_call(functools.partial(kernel, slabs), out_shape=(gi_shape, jax...]
where the time goes in v2:
time: 49.9 us; the launch traced here: 49.1 us
  Pallas kernels  48.5 us (97%)
  between operations  0.64 us (1%)
    pallas_call x1, Pallas kernels, local(): pl.pallas_call(functools.partial(kernel, slabs), out_shape=(gi_shape, jax...  45.1 us
    pallas_call x1, Pallas kernels, local(): pl.pallas_call(functools.partial(finish, slabs), out_shape=(gi_shape, jax...  3.38 us

profile of v2, /device:TPU:1, one launch (start us, length us, event | category | flops | bytes accessed | tf_op | source)
XLA Modules:
  0.0 49.1 jit_solution(15107459306825662758)
XLA Ops:
  0.6 45.1 %shard_map.130 = (f32[6,384,128]{2,1,0:T(8,128)}, bf16[2,16,64,128]{3,2,1,0:T(8,128)(2,1)}) custom-call(bf16[6,384,128]{2,1,0:T(8,128)(2,1)} %bitcast.7, bf16[2,384,128]{2,1,0:T(8,128)(2,1)} %bitcast.8, bf16[2,384,128]{2,1,0:T(8,128)(2,1)} %bitcast.9, f32[1,96]{1,0:T(1,128)} %bitcast.11, f32[1,96]{1,0:T(1,128)} %bitcast.12, ...), custom_call_target="tpu_custom_call" | custom-call | tf_op jit(solution)/shard_map/pallas_call | solution.py:657
  45.7 3.4 %shard_map.131 = (f32[6,384,128]{2,1,0:T(8,128)}, f32[3,3,3,96,96]{4,3,2,1,0:T(8,128)}, f32[3,3,3,3,96]{4,3,2,1,0:T(4,128)}) custom-call(f32[6,384,128]{2,1,0:T(8,128)} %get-tuple-element.8.gi_hbm, bf16[2,16,64,128]{3,2,1,0:T(8,128)(2,1)} %get-tuple-element.9.sums_hbm), custom_call_target="tpu_custom_call" | custom-call | tf_op jit(solution)/shard_map/pallas_call | solution.py:721

commit v3 on v2

--- a/solution.py
+++ b/solution.py
@@ -75,8 +75,8 @@
     tab_hbm,
     idx_hbm,
     ord_hbm,
-    gi_hbm,
-    sums_hbm,
+    gi_ref,
+    sums_ref,
     x_ref,
     mc_ref,
     hc_ref,
@@ -88,7 +88,6 @@
     tab_ref,
     idx_ref,
     ord_ref,
-    gi_ref,
     stage,
     xs,
     gains,
@@ -122,7 +121,6 @@
     got3,
     full,
     ins,
-    outs,
     hs,
     hr,
     ps,
@@ -211,15 +209,30 @@
             up if side == 0 else down,
         )
 
+    groups = (slice(0, 4), slice(4, 6), slice(6, 8))
+
     def hin_copy(side, f):
+        group = 0 if f < 4 else 1 if f < 6 else 2
         if side == 0:
-            return remote(hin.at[f, :, pl.ds(0, COLS)], hin_b.at[f], hs.at[0, f], hr.at[1, f], up)
-        return remote(hin.at[f, :, pl.ds(3 * COLS, COLS)], hin_t.at[f], hs.at[1, f], hr.at[0, f], down)
+            row, there = hin.at[f, :, pl.ds(0, COLS)], hin_b.at[f]
+            return remote(row, there, hs.at[0], hr.at[1, group], up)
+        row, there = hin.at[f, :, pl.ds(3 * COLS, COLS)], hin_t.at[f]
+        return remote(row, there, hs.at[1], hr.at[0, group], down)
+
+    def whole(ref, send, recv):
+        return remote(ref, ref, send, recv, sibling)
 
     def dob_copy(side, f):
         if side == 0:
-            return remote(dob.at[f, :, pl.ds(0, COLS)], dob_b.at[f], ds.at[0, f], dr.at[1, f], up)
-        return remote(dob.at[f, :, pl.ds(3 * COLS, COLS)], dob_t.at[f], ds.at[1, f], dr.at[0, f], down)
+            row, there = dob.at[f, :, pl.ds(0, COLS)], dob_b.at[f]
+            return remote(row, there, ds.at[0], dr.at[1], up)
+        row, there = dob.at[f, :, pl.ds(3 * COLS, COLS)], dob_t.at[f]
+        return remote(row, there, ds.at[1], dr.at[0], down)
+
+    pl.semaphore_wait(barrier, planes + 2)
+    for j in range(2):
+        for side in range(2):
+            hin_copy(side, j).start()
 
     for n in (7, 8, 9, 10):
         loads[n].wait()
@@ -244,12 +257,8 @@
     loads[0].wait()
     loads[3].wait()
     gains[0] = jnp.broadcast_to(gin_ref[...], (COLS, C)).T
-    pl.semaphore_wait(barrier, planes + 2)
     for side in range(2):
         pg_copy(side).start()
-    for j in range(2):
-        for side in range(2):
-            hin_copy(side, j).start()
 
     def make_h(f):
         value = split_rows(f, x_ref[f])
@@ -389,13 +398,12 @@
         jnp.concatenate([head[f, :, COLS : 3 * COLS] for f in range(8)], axis=1),
     )
 
-    def hin_arrived(frames):
-        for f in frames:
-            for side in range(2):
-                hin_copy(side, f).wait_recv()
-
-        some = slice(frames[0], frames[-1] + 1)
-        shape = (len(frames), C, COLS)
+    def hin_arrived(group):
+        some = groups[group]
+        shape = (some.stop - some.start, C, COLS)
+        span = pl.ds(some.start, shape[0])
+        whole(hin_t.at[span], hs.at[1], hr.at[0, group]).wait_recv()
+        whole(hin_b.at[span], hs.at[0], hr.at[1, group]).wait_recv()
 
         @pl.when(me == 0)
         def _():
@@ -424,25 +432,22 @@
         image = jnp.concatenate([xs[f, :, 0:COLS], xs[f, :, 3 * COLS : 4 * COLS]], axis=1)
         finish_out(f, (0, 3), image, conv, cot, dsh_edge)
 
-    early = range(0, 4)
     late = range(4, FR)
-    hin_arrived(range(0, 6))
-    for f in early:
-        forward_edges(f)
-    for f in early:
-        for side in range(2):
-            dob_copy(side, f).start()
-    part = dot_nt(
-        jnp.concatenate([edge_grads(0, early), edge_grads(1, early)], axis=0), edge_windows(early)
-    )
-    mid_grads[0] += part[0 : 3 * C // 2]
-    mid_grads[1] += part[3 * C // 2 : 3 * C]
-    hin_arrived(range(6, 8))
-    for f in late:
-        forward_edges(f)
-    for f in late:
-        for side in range(2):
-            dob_copy(side, f).start()
+    for group in range(3):
+        frames = range(2 * group, 2 * group + 2)
+        hin_arrived(group)
+        for f in frames:
+            forward_edges(f)
+        for f in frames:
+            for side in range(2):
+                dob_copy(side, f).start()
+        if group < 2:
+            part = dot_nt(
+                jnp.concatenate([edge_grads(0, frames), edge_grads(1, frames)], axis=0),
+                edge_windows(frames),
+            )
+            mid_grads[0] += part[0 : 3 * C // 2]
+            mid_grads[1] += part[3 * C // 2 : 3 * C]
 
     total = head_mid[...] + dot_nt(
         jnp.concatenate([head_edge_taps(f) for f in range(8)], axis=1),
@@ -471,18 +476,18 @@
         return remote(piece, got1, s1, r1, sibling)
 
     def scatter_copy(k):
-        return remote(sum1.at[(xy + k) % planes], got2.at[k], s2.at[k], r2.at[k], in_plane(k))
+        return remote(sum1.at[(xy + k) % planes], got2.at[k], s2, r2, in_plane(k))
 
     def z_copy():
         return remote(half3, got3, s3, r3, zpartner)
 
     def gather_copy(k):
         mine = full.at[core, xy]
-        return remote(mine, mine, s4.at[k], r4.at[k], in_plane(k))
+        return remote(mine, mine, s4, r4.at[k // 4], in_plane(k))
 
     def pass_on(k):
         one = full.at[core, (xy + planes - k) % planes]
-        return remote(one, one, s5.at[k], r5.at[k], sibling)
+        return remote(one, one, s5, r5, sibling)
 
     half_grads(1 - core)
     for tile in range(64):
@@ -528,16 +533,14 @@
         backward_middle(f)
 
     total = sum1[xy].astype(F32)
-    for k in range(1, planes):
-        scatter_copy(k).wait_recv()
+    whole(got2.at[pl.ds(1, planes - 1)], s2, r2).wait_recv()
     for k in range(1, planes):
         total = total + got2[k].astype(F32)
     half3[...] = total.astype(BF16)
     z_copy().start()
 
-    for f in range(FR):
-        for side in range(2):
-            dob_copy(side, f).wait_recv()
+    whole(dob_t.at[pl.ds(0, FR)], ds.at[1], dr.at[0]).wait_recv()
+    whole(dob_b.at[pl.ds(0, FR)], ds.at[0], dr.at[1]).wait_recv()
 
     @pl.when(me == 0)
     def _():
@@ -549,53 +552,37 @@
 
     for f in range(0, FR):
         backward_edges(f)
-    store = pltpu.make_async_copy(gi_ref, gi_hbm, outs.at[0])
-    store.start()
 
     z_copy().wait_recv()
     full[core, xy] = (half3[...].astype(F32) + got3[...].astype(F32)).astype(BF16)
     for k in range(1, planes):
         gather_copy(k).start()
     pass_on(0).start()
-    for k in range(1, planes):
-        gather_copy(k).wait_recv()
-        pass_on(k).start()
-    own = pltpu.make_async_copy(full.at[core], sums_hbm.at[core], outs.at[1])
-    own.start()
-    for k in range(planes):
-        pass_on(k).wait_recv()
-    other = pltpu.make_async_copy(full.at[1 - core], sums_hbm.at[1 - core], outs.at[2])
-    other.start()
+    for low in range(0, planes, 4):
+        some = range(max(low, 1), min(low + 4, planes))
+        whole(got2.at[pl.ds(0, len(some))], s4, r4.at[low // 4]).wait_recv()
+        for k in some:
+            pass_on(k).start()
+    whole(full.at[1 - core], s5, r5).wait_recv()
+    sums_ref[...] = full[...]
 
     for side in range(2):
         pg_copy(side).wait_send()
-        for f in range(8):
-            hin_copy(side, f).wait_send()
-        for f in range(FR):
-            dob_copy(side, f).wait_send()
+        whole(hin_t, hs.at[side], hr.at[side, 0]).wait_send()
+        whole(dob_t.at[pl.ds(0, FR)], ds.at[side], dr.at[side]).wait_send()
     pair_copy().wait_send()
+    whole(got2.at[pl.ds(1, planes - 1)], s2, r2).wait_send()
     z_copy().wait_send()
-    pass_on(0).wait_send()
-    for k in range(1, planes):
-        scatter_copy(k).wait_send()
-        gather_copy(k).wait_send()
-        pass_on(k).wait_send()
-    store.wait()
-    own.wait()
-    other.wait()
-
-
-def finish(slabs, gi_hbm, sums_hbm, out_hbm, gm_hbm, gh_ref, gi, sums, grads, gm, ins, outs):
-    sums_in = pltpu.make_async_copy(sums_hbm, sums, ins.at[FR])
-    sums_in.start()
-    gi_in = [pltpu.make_async_copy(gi_hbm.at[f], gi.at[f], ins.at[f]) for f in range(FR)]
-    gi_out = [pltpu.make_async_copy(gi.at[f], out_hbm.at[f], outs.at[f]) for f in range(FR)]
-    for copy in gi_in:
-        copy.start()
+    whole(got2.at[pl.ds(1, planes - 1)], s4, r4.at[0]).wait_send()
+    whole(full.at[core], s5, r5).wait_send()
+
+
+def finish(slabs, gi_ref, sums, out_hbm, gm_hbm, gh_hbm, grads, gm, gh, outs):
+    gi_out = pltpu.make_async_copy(gi_ref, out_hbm, outs.at[3])
+    gi_out.start()
     planes = slabs // 4
     per = 64 // planes
     scale = (1.0 / (FR * slabs * 4 * COLS)) ** 0.5
-    sums_in.wait()
     for half in range(2):
         for tile in range(63):
             owner, k = divmod(tile, per)
@@ -603,16 +590,13 @@
             at = half * (3 * C // 2) + row * 16
             value = sums[half, owner, k * 16 : (k + 1) * 16].astype(F32) * scale
             grads[at : at + 16, lane * COLS : (lane + 1) * COLS] = value
-    for f in range(FR):
-        gi_in[f].wait()
-        gi_out[f].start()
     gm_out = []
     for t in range(3):
         for y in range(3):
             for x in range(3):
                 at = (y * 3 + t) * C
                 gm[t, y, x] = grads[x * C : (x + 1) * C, at : at + C]
-        gm_out.append(pltpu.make_async_copy(gm.at[t], gm_hbm.at[t], outs.at[FR + t]))
+        gm_out.append(pltpu.make_async_copy(gm.at[t], gm_hbm.at[t], outs.at[t]))
         gm_out[t].start()
     head = []
     for half in range(2):
@@ -626,8 +610,10 @@
         for x in range(3):
             for t in range(3):
                 at = y * 32 + x * 9 + t * 3
-                gh_ref[2 - t, y, x] = head[at : at + 3, :]
-    for copy in gi_out + gm_out:
+                gh[2 - t, y, x] = head[at : at + 3, :]
+    gh_out = pltpu.make_async_copy(gh, gh_hbm, outs.at[4])
+    gh_out.start()
+    for copy in [gi_out, gh_out] + gm_out:
         copy.wait()
 
 
@@ -636,7 +622,6 @@
     planes = slabs // 4
     unit = (1024 // planes, COLS)
     plane = (planes,) + unit
-    anywhere = pl.BlockSpec(memory_space=pl.ANY)
     hbm = pl.BlockSpec(memory_space=pltpu.HBM)
     vmem = pl.BlockSpec(memory_space=pltpu.VMEM)
     dma = pltpu.SemaphoreType.DMA
@@ -656,13 +641,12 @@
     gi_shape = jax.ShapeDtypeStruct((FR, 4 * C, COLS), F32)
     gi, sums = pl.pallas_call(
         functools.partial(kernel, slabs),
-        out_shape=(gi_shape, jax.ShapeDtypeStruct((2,) + plane, BF16)),
-        in_specs=[anywhere] * 11,
-        out_specs=[anywhere] * 2,
+        out_shape=(pltpu.VMEM(gi_shape.shape, F32), pltpu.VMEM((2,) + plane, BF16)),
+        in_specs=[hbm] * 11,
+        out_specs=[vmem] * 2,
         scratch_shapes=[pltpu.VMEM(value.shape, value.dtype) for value in operands[:8]]
         + [pltpu.SMEM(value.shape, value.dtype) for value in operands[8:]]
         + [
-            pltpu.VMEM((FR, 4 * C, COLS), F32),
             pltpu.VMEM((FR, 4 * C, COLS), F32),
             pltpu.VMEM((FR, C, 4 * COLS), F32),
             pltpu.VMEM((2, C, COLS), F32),
@@ -696,23 +680,22 @@
             pltpu.VMEM(unit, BF16),
             pltpu.VMEM((2,) + plane, BF16),
             dma((11,)),
-            dma((3,)),
-            dma((2, 8)),
-            dma((2, 8)),
+            dma((2,)),
+            dma((2, 3)),
             dma((2,)),
             dma((2,)),
-            dma((2, FR)),
-            dma((2, FR)),
-            dma,
-            dma,
-            dma((planes,)),
-            dma((planes,)),
-            dma,
-            dma,
-            dma((planes,)),
-            dma((planes,)),
-            dma((planes,)),
-            dma((planes,)),
+            dma((2,)),
+            dma((2,)),
+            dma,
+            dma,
+            dma,
+            dma,
+            dma,
+            dma,
+            dma,
+            dma(((planes + 3) // 4,)),
+            dma,
+            dma,
         ],
         compiler_params=pltpu.CompilerParams(
             collective_id=0, has_side_effects=True, vmem_limit_bytes=56 * 2**20
@@ -725,17 +708,15 @@
             jax.ShapeDtypeStruct((3, 3, 3, C, C), F32),
             jax.ShapeDtypeStruct((3, 3, 3, 3, C), F32),
         ),
-        in_specs=[hbm, hbm],
-        out_specs=[hbm, hbm, vmem],
+        in_specs=[vmem, vmem],
+        out_specs=[hbm, hbm, hbm],
         scratch_shapes=[
-            pltpu.VMEM((FR, 4 * C, COLS), F32),
-            pltpu.VMEM((2,) + plane, BF16),
             pltpu.VMEM((3 * C, 7 * COLS), F32),
             pltpu.VMEM((3, 3, 3, C, C), F32),
-            dma((FR + 1,)),
-            dma((FR + 3,)),
+            pltpu.VMEM((3, 3, 3, 3, C), F32),
+            dma((5,)),
         ],
-        compiler_params=pltpu.CompilerParams(vmem_limit_bytes=60 * 2**20),
+        compiler_params=pltpu.CompilerParams(vmem_limit_bytes=16 * 2**20),
     )(gi, sums)
     return gi.reshape(FR, C, 4, COLS), gm, gh
 

time: 49.9 us -> 45.1 us (0.904); the launches traced: 49.1 us -> 45 us
  Pallas kernels: 48.5 us -> 44.3 us
    pallas_call x1, Pallas kernels: 45.1 us -> 42.9 us  [local(): pl.pallas_call(functools.partial(kernel, slabs), out_shape=(pltpu.VMEM(gi...]
    pallas_call x1, Pallas kernels: 3.38 us -> 1.49 us  [local(): pl.pallas_call(functools.partial(finish, slabs), out_shape=(gi_shape, jax...]
where the time goes in v3:
time: 45.1 us; the launch traced here: 45 us
  Pallas kernels  44.3 us (98%)
  between operations  0.64 us (1%)
    pallas_call x1, Pallas kernels, local(): pl.pallas_call(functools.partial(kernel, slabs), out_shape=(pltpu.VMEM(gi...  42.9 us
    pallas_call x1, Pallas kernels, local(): pl.pallas_call(functools.partial(finish, slabs), out_shape=(gi_shape, jax...  1.49 us

profile of v3, /device:TPU:1, one launch (start us, length us, event | category | flops | bytes accessed | tf_op | source)
XLA Modules:
  0.0 45.0 jit_solution(15581708067982001871)
XLA Ops:
  0.6 42.9 %shard_map.130 = (f32[6,384,128]{2,1,0:T(8,128)S(1)}, bf16[2,16,64,128]{3,2,1,0:T(8,128)(2,1)S(1)}) custom-call(bf16[6,384,128]{2,1,0:T(8,128)(2,1)} %bitcast.7, bf16[2,384,128]{2,1,0:T(8,128)(2,1)} %bitcast.8, bf16[2,384,128]{2,1,0:T(8,128)(2,1)} %bitcast.9, f32[1,96]{1,0:T(1,128)} %bitcast.11, f32[1,96]{1,0:T(1,128)} %bitcast.12, ...), custom_call_target="tpu_custom_call" | custom-call | tf_op jit(solution)/shard_map/pallas_call | solution.py:642
  43.5 1.5 %shard_map.131 = (f32[6,384,128]{2,1,0:T(8,128)}, f32[3,3,3,96,96]{4,3,2,1,0:T(8,128)}, f32[3,3,3,3,96]{4,3,2,1,0:T(4,128)}) custom-call(f32[6,384,128]{2,1,0:T(8,128)S(1)} %get-tuple-element.8.gi_ref, bf16[2,16,64,128]{3,2,1,0:T(8,128)(2,1)S(1)} %get-tuple-element.9.sums), custom_call_target="tpu_custom_call" | custom-call | tf_op jit(solution)/shard_map/pallas_call | solution.py:704

commit v4 on v3

--- a/solution.py
+++ b/solution.py
@@ -60,6 +60,17 @@
     inner = cot * gain * (sig * (1.0 + normed * (1.0 - sig)))
     mean = jnp.sum(inner * unit, axis=0, keepdims=True) * (1.0 / C)
     return root * (inner - unit * mean)
+
+
+def tiles_of(core):
+    return range(0, 16) if core == 0 else range(16, 128)
+
+
+def where_is(planes, tile):
+    core = 0 if tile < 16 else 1
+    tiles = tiles_of(core)
+    owner, k = divmod(tile - tiles[0], len(tiles) // planes)
+    return owner, slice(k * 16, (k + 1) * 16)
 
 
 def kernel(
@@ -76,7 +87,8 @@
     idx_hbm,
     ord_hbm,
     gi_ref,
-    sums_ref,
+    sums0_ref,
+    sums1_ref,
     x_ref,
     mc_ref,
     hc_ref,
@@ -111,15 +123,21 @@
     dsh_edge,
     mid_grads,
     head_mid,
-    head_sum,
     grads,
-    piece,
-    got1,
-    sum1,
-    got2,
-    half3,
-    got3,
-    full,
+    piece0,
+    piece1,
+    got10,
+    got11,
+    sum10,
+    sum11,
+    got20,
+    got21,
+    half30,
+    half31,
+    got30,
+    got31,
+    full0,
+    full1,
     ins,
     hs,
     hr,
@@ -143,14 +161,35 @@
     place = me % 4
     zh = place // 2
     xy = me // 4
+    piece = (piece0, piece1)
+    got1 = (got10, got11)
+    sum1 = (sum10, sum11)
+    got2 = (got20, got21)
+    half3 = (half30, half31)
+    got3 = (got30, got31)
+    full = (full0, full1)
     planes = slabs // 4
     up = (me + slabs - 1) % slabs
     down = (me + 1) % slabs
     sibling = me + 1 - 2 * core
     zpartner = me + 2 - 4 * zh
 
+    side_len = int(planes**0.5)
+    px, py = xy % side_len, xy // side_len
+    offsets = [(a, b) for a in range(side_len) for b in range(side_len)]
+    offsets.sort(key=lambda at: -sum(min(step, side_len - step) for step in at))
+    offsets = offsets[-1:] + offsets[:-1]
+
+    def chip_at(k):
+        a, b = offsets[k]
+        return (py + a) % side_len * side_len + (px + b) % side_len
+
+    def chip_from(k):
+        a, b = offsets[k]
+        return (py + side_len - a) % side_len * side_len + (px + side_len - b) % side_len
+
     def in_plane(k):
-        return ((xy + k) % planes) * 4 + place
+        return chip_at(k) * 4 + place
 
     pairs = (
         (x_hbm, x_ref),
@@ -182,12 +221,13 @@
     def greet(to):
         pl.semaphore_signal(barrier, inc=1, device_id={"slab": to}, device_id_type=MESH)
 
+    loads[1].start()
     greet(up)
     greet(down)
     greet(zpartner)
     for k in range(1, planes):
         greet(in_plane(k))
-    for n in (1, 0, 3, 8, 9, 10, 7, 2, 5, 6, 4):
+    for n in (0, 3, 8, 9, 10, 7, 2, 5, 6, 4):
         loads[n].start()
 
     def split_rows(f, source):
@@ -453,49 +493,91 @@
         jnp.concatenate([head_edge_taps(f) for f in range(8)], axis=1),
         jnp.concatenate([head_edges(f) for f in range(8)], axis=1),
     )
-    head_sum[0] = total[0 : C // 2]
-    head_sum[1] = total[C // 2 : C]
-
-    per = 64 // planes
-
-    def where_is(tile):
-        owner, k = divmod(tile, per)
-        return owner, slice(k * 16, (k + 1) * 16)
+    part = dot_nt(
+        jnp.concatenate([edge_grads(0, late), edge_grads(1, late)], axis=0), edge_windows(late)
+    )
+    for half in range(2):
+        rows = slice(half * (3 * C // 2), (half + 1) * (3 * C // 2))
+        grads[rows, 0:K3] = mid_grads[half] + part[rows]
+    for n in range(3):
+        grads[n * C : (n + 1) * C, K3 : K3 + 32] = total[:, n * 32 : (n + 1) * 32]
 
     def tile_of(tile):
         row, lane = divmod(tile, 7)
         return grads[row * 16 : (row + 1) * 16, lane * COLS : (lane + 1) * COLS]
 
-    def half_grads(half):
-        grads[:, 0:K3] = mid_grads[half] + dot_nt(edge_grads(half, late), edge_windows(late))
-        for n in range(3):
-            rows = slice(n * (C // 2), (n + 1) * (C // 2))
-            grads[rows, K3 : K3 + 32] = head_sum[half, :, n * 32 : (n + 1) * 32]
-
-    def pair_copy():
-        return remote(piece, got1, s1, r1, sibling)
-
-    def scatter_copy(k):
-        return remote(sum1.at[(xy + k) % planes], got2.at[k], s2, r2, in_plane(k))
-
-    def z_copy():
-        return remote(half3, got3, s3, r3, zpartner)
-
-    def gather_copy(k):
-        mine = full.at[core, xy]
+    def pair_copy(c):
+        return remote(piece[1 - c], got1[1 - c], s1, r1, sibling)
+
+    def scatter_copy(c, k):
+        part = sum1[c].at[chip_at(k)]
+        return remote(part, got2[c].at[k], s2, r2, in_plane(k))
+
+    def z_copy(c):
+        return remote(half3[c], got3[c], s3, r3, zpartner)
+
+    def gather_copy(c, k):
+        mine = full[c].at[xy]
         return remote(mine, mine, s4, r4.at[k // 4], in_plane(k))
 
-    def pass_on(k):
-        one = full.at[core, (xy + planes - k) % planes]
+    def pass_on(c, k):
+        one = full[c].at[chip_from(k)]
         return remote(one, one, s5, r5, sibling)
 
-    half_grads(1 - core)
-    for tile in range(64):
-        owner, rows = where_is(tile)
-        value = tile_of(tile).astype(BF16) if tile < 63 else jnp.zeros((16, COLS), BF16)
-        piece[owner, rows] = value
-    pair_copy().start()
-    half_grads(core)
+    def others(c):
+        return got2[c].at[pl.ds(1, planes - 1)]
+
+    def on_core(stage):
+        for c in range(2):
+            pl.when(core == c)(functools.partial(stage, c))
+
+    def start_pair(c):
+        for tile in tiles_of(1 - c):
+            owner, rows = where_is(planes, tile)
+            value = tile_of(tile).astype(BF16) if tile < 126 else jnp.zeros((16, COLS), BF16)
+            piece[1 - c][owner, rows] = value
+        pair_copy(c).start()
+
+    def start_scatter(c):
+        whole(got1[c], s1, r1).wait_recv()
+        for tile in tiles_of(c):
+            owner, rows = where_is(planes, tile)
+            value = got1[c][owner, rows].astype(F32)
+            if tile < 126:
+                value = value + tile_of(tile)
+            sum1[c][owner, rows] = value.astype(BF16)
+        for k in range(1, planes):
+            scatter_copy(c, k).start()
+
+    def start_z(c):
+        whole(others(c), s2, r2).wait_recv()
+        total = sum1[c][xy].astype(F32)
+        for k in range(1, planes):
+            total = total + got2[c][k].astype(F32)
+        half3[c][...] = total.astype(BF16)
+        z_copy(c).start()
+
+    def gather(c):
+        z_copy(c).wait_recv()
+        full[c][xy] = (half3[c][...].astype(F32) + got3[c][...].astype(F32)).astype(BF16)
+        for k in range(1, planes):
+            gather_copy(c, k).start()
+        pass_on(c, 0).start()
+        for low in range(0, planes, 4):
+            some = range(max(low, 1), min(low + 4, planes))
+            whole(got2[c].at[pl.ds(0, len(some))], s4, r4.at[low // 4]).wait_recv()
+            for k in some:
+                pass_on(c, k).start()
+        whole(full[1 - c], s5, r5).wait_recv()
+
+    def sums_left(c):
+        pair_copy(c).wait_send()
+        whole(others(c), s2, r2).wait_send()
+        z_copy(c).wait_send()
+        whole(others(c), s4, r4.at[0]).wait_send()
+        whole(full[c], s5, r5).wait_send()
+
+    on_core(start_pair)
 
     dob[6] = jnp.zeros((C, 4 * COLS), BF16)
     dob[7] = jnp.zeros((C, 4 * COLS), BF16)
@@ -519,25 +601,12 @@
         window = edges_of(dob, dob_t, dob_b, f)
         finish_in(f, (0, 3), columns(dot(wt[...], window), earlier, later))
 
-    pair_copy().wait_recv()
-    for tile in range(64):
-        owner, rows = where_is(tile)
-        value = got1[owner, rows].astype(F32)
-        if tile < 63:
-            value = value + tile_of(tile)
-        sum1[owner, rows] = value.astype(BF16)
-    for k in range(1, planes):
-        scatter_copy(k).start()
+    on_core(start_scatter)
 
     for f in range(0, FR):
         backward_middle(f)
 
-    total = sum1[xy].astype(F32)
-    whole(got2.at[pl.ds(1, planes - 1)], s2, r2).wait_recv()
-    for k in range(1, planes):
-        total = total + got2[k].astype(F32)
-    half3[...] = total.astype(BF16)
-    z_copy().start()
+    on_core(start_z)
 
     whole(dob_t.at[pl.ds(0, FR)], ds.at[1], dr.at[0]).wait_recv()
     whole(dob_b.at[pl.ds(0, FR)], ds.at[0], dr.at[1]).wait_recv()
@@ -553,43 +622,29 @@
     for f in range(0, FR):
         backward_edges(f)
 
-    z_copy().wait_recv()
-    full[core, xy] = (half3[...].astype(F32) + got3[...].astype(F32)).astype(BF16)
-    for k in range(1, planes):
-        gather_copy(k).start()
-    pass_on(0).start()
-    for low in range(0, planes, 4):
-        some = range(max(low, 1), min(low + 4, planes))
-        whole(got2.at[pl.ds(0, len(some))], s4, r4.at[low // 4]).wait_recv()
-        for k in some:
-            pass_on(k).start()
-    whole(full.at[1 - core], s5, r5).wait_recv()
-    sums_ref[...] = full[...]
+    on_core(gather)
+    sums0_ref[...] = full[0][...]
+    sums1_ref[...] = full[1][...]
 
     for side in range(2):
         pg_copy(side).wait_send()
         whole(hin_t, hs.at[side], hr.at[side, 0]).wait_send()
         whole(dob_t.at[pl.ds(0, FR)], ds.at[side], dr.at[side]).wait_send()
-    pair_copy().wait_send()
-    whole(got2.at[pl.ds(1, planes - 1)], s2, r2).wait_send()
-    z_copy().wait_send()
-    whole(got2.at[pl.ds(1, planes - 1)], s4, r4.at[0]).wait_send()
-    whole(full.at[core], s5, r5).wait_send()
-
-
-def finish(slabs, gi_ref, sums, out_hbm, gm_hbm, gh_hbm, grads, gm, gh, outs):
+    on_core(sums_left)
+
+
+def finish(slabs, gi_ref, sums0, sums1, out_hbm, gm_hbm, gh_hbm, grads, gm, gh, outs):
     gi_out = pltpu.make_async_copy(gi_ref, out_hbm, outs.at[3])
     gi_out.start()
     planes = slabs // 4
-    per = 64 // planes
     scale = (1.0 / (FR * slabs * 4 * COLS)) ** 0.5
-    for half in range(2):
-        for tile in range(63):
-            owner, k = divmod(tile, per)
-            row, lane = divmod(tile, 7)
-            at = half * (3 * C // 2) + row * 16
-            value = sums[half, owner, k * 16 : (k + 1) * 16].astype(F32) * scale
-            grads[at : at + 16, lane * COLS : (lane + 1) * COLS] = value
+    for c, sums in enumerate((sums0, sums1)):
+        for tile in tiles_of(c):
+            if tile < 126:
+                owner, rows = where_is(planes, tile)
+                row, lane = divmod(tile, 7)
+                value = sums[owner, rows].astype(F32) * scale
+                grads[row * 16 : (row + 1) * 16, lane * COLS : (lane + 1) * COLS] = value
     gm_out = []
     for t in range(3):
         for y in range(3):
@@ -598,14 +653,7 @@
                 gm[t, y, x] = grads[x * C : (x + 1) * C, at : at + C]
         gm_out.append(pltpu.make_async_copy(gm.at[t], gm_hbm.at[t], outs.at[t]))
         gm_out[t].start()
-    head = []
-    for half in range(2):
-        top = half * (3 * C // 2)
-        parts = [
-            grads[top + n * (C // 2) : top + (n + 1) * (C // 2), K3 : K3 + 32] for n in range(3)
-        ]
-        head.append(jnp.concatenate(parts, axis=1))
-    head = jnp.concatenate(head, axis=0)
+    head = jnp.concatenate([grads[n * C : (n + 1) * C, K3 : K3 + 32] for n in range(3)], axis=1)
     for y in range(3):
         for x in range(3):
             for t in range(3):
@@ -620,8 +668,7 @@
 def local(slabs, *operands):
     (x, mc, hc, gin, gout, mw, hw, ag, tab, idx, order) = operands
     planes = slabs // 4
-    unit = (1024 // planes, COLS)
-    plane = (planes,) + unit
+    share = [(planes, 16 * len(tiles_of(c)) // planes, COLS) for c in range(2)]
     hbm = pl.BlockSpec(memory_space=pltpu.HBM)
     vmem = pl.BlockSpec(memory_space=pltpu.VMEM)
     dma = pltpu.SemaphoreType.DMA
@@ -639,11 +686,13 @@
         order,
     )
     gi_shape = jax.ShapeDtypeStruct((FR, 4 * C, COLS), F32)
-    gi, sums = pl.pallas_call(
+    gi, sums0, sums1 = pl.pallas_call(
         functools.partial(kernel, slabs),
-        out_shape=(pltpu.VMEM(gi_shape.shape, F32), pltpu.VMEM((2,) + plane, BF16)),
+        out_shape=(pltpu.VMEM(gi_shape.shape, F32),) + tuple(
+            pltpu.VMEM(plane, BF16) for plane in share
+        ),
         in_specs=[hbm] * 11,
-        out_specs=[vmem] * 2,
+        out_specs=[vmem] * 3,
         scratch_shapes=[pltpu.VMEM(value.shape, value.dtype) for value in operands[:8]]
         + [pltpu.SMEM(value.shape, value.dtype) for value in operands[8:]]
         + [
@@ -670,15 +719,10 @@
             pltpu.VMEM((2, FR, 3 * C // 2, 2 * COLS), BF16),
             pltpu.VMEM((2, 3 * C // 2, K3), F32),
             pltpu.VMEM((C, C), F32),
-            pltpu.VMEM((2, C // 2, C), F32),
-            pltpu.VMEM((3 * C // 2, 7 * COLS), F32),
-            pltpu.VMEM(plane, BF16),
-            pltpu.VMEM(plane, BF16),
-            pltpu.VMEM(plane, BF16),
-            pltpu.VMEM(plane, BF16),
-            pltpu.VMEM(unit, BF16),
-            pltpu.VMEM(unit, BF16),
-            pltpu.VMEM((2,) + plane, BF16),
+            pltpu.VMEM((3 * C, 7 * COLS), F32),
+            *[pltpu.VMEM(plane, BF16) for _ in range(4) for plane in share],
+            *[pltpu.VMEM(plane[1:], BF16) for _ in range(2) for plane in share],
+            *[pltpu.VMEM(plane, BF16) for plane in share],
             dma((11,)),
             dma((2,)),
             dma((2, 3)),
@@ -708,7 +752,7 @@
             jax.ShapeDtypeStruct((3, 3, 3, C, C), F32),
             jax.ShapeDtypeStruct((3, 3, 3, 3, C), F32),
         ),
-        in_specs=[vmem, vmem],
+        in_specs=[vmem] * 3,
         out_specs=[hbm, hbm, hbm],
         scratch_shapes=[
             pltpu.VMEM((3 * C, 7 * COLS), F32),
@@ -717,7 +761,7 @@
             dma((5,)),
         ],
         compiler_params=pltpu.CompilerParams(vmem_limit_bytes=16 * 2**20),
-    )(gi, sums)
+    )(gi, sums0, sums1)
     return gi.reshape(FR, C, 4, COLS), gm, gh
 
 

time: 45.1 us -> 44.2 us (0.980)
  Pallas kernels: 44.3 us -> 43.3 us
    pallas_call x1, Pallas kernels: 42.9 us -> 41.8 us  [local(): pl.pallas_call(functools.partial(kernel, slabs), out_shape=(pltpu.VMEM(gi...]
where the time goes in v4:
time: 44.2 us; the launch traced here: 43.9 us
  Pallas kernels  43.3 us (98%)
  between operations  0.64 us (1%)
    pallas_call x1, Pallas kernels, local(): pl.pallas_call(functools.partial(kernel, slabs), out_shape=(pltpu.VMEM(gi...  41.8 us
    pallas_call x1, Pallas kernels, local(): pl.pallas_call(functools.partial(finish, slabs), out_shape=(gi_shape, jax...  1.49 us

profile of v4, /device:TPU:1, one launch (start us, length us, event | category | flops | bytes accessed | tf_op | source)
XLA Modules:
  0.0 43.9 jit_solution(13087913931233185294)
XLA Ops:
  0.6 41.8 %shard_map.130 = (f32[6,384,128]{2,1,0:T(8,128)S(1)}, bf16[16,16,128]{2,1,0:T(8,128)(2,1)S(1)}, bf16[16,112,128]{2,1,0:T(8,128)(2,1)S(1)}) custom-call(bf16[6,384,128]{2,1,0:T(8,128)(2,1)} %bitcast.7, bf16[2,384,128]{2,1,0:T(8,128)(2,1)} %bitcast.8, bf16[2,384,128]{2,1,0:T(8,128)(2,1)} %bitcast.9, f32[1,96]{1,0:T(1,128)} %bitcast.11, f32[1,96]{1,0:T(1,128)} %bitcast.12, ...), custom_call_target="tpu_custom_call" | custom-call | tf_op jit(solution)/shard_map/pallas_call | solution.py:689
  42.4 1.5 %shard_map.131 = (f32[6,384,128]{2,1,0:T(8,128)}, f32[3,3,3,96,96]{4,3,2,1,0:T(8,128)}, f32[3,3,3,3,96]{4,3,2,1,0:T(4,128)}) custom-call(f32[6,384,128]{2,1,0:T(8,128)S(1)} %get-tuple-element.9.gi_ref, bf16[16,16,128]{2,1,0:T(8,128)(2,1)S(1)} %get-tuple-element.10.sums0, bf16[16,112,128]{2,1,0:T(8,128)(2,1)S(1)} %get-tuple-element.11.sums1), custom_call_target="tpu_custom_call" | custom-call | tf_op jit(solution)/shard_map/pallas_call | solution.py:748

commit v5 on v4

--- a/solution.py
+++ b/solution.py
@@ -472,6 +472,12 @@
         image = jnp.concatenate([xs[f, :, 0:COLS], xs[f, :, 3 * COLS : 4 * COLS]], axis=1)
         finish_out(f, (0, 3), image, conv, cot, dsh_edge)
 
+    def head_part(frames):
+        return dot_nt(
+            jnp.concatenate([head_edge_taps(f) for f in frames], axis=1),
+            jnp.concatenate([head_edges(f) for f in frames], axis=1),
+        )
+
     late = range(4, FR)
     for group in range(3):
         frames = range(2 * group, 2 * group + 2)
@@ -488,11 +494,10 @@
             )
             mid_grads[0] += part[0 : 3 * C // 2]
             mid_grads[1] += part[3 * C // 2 : 3 * C]
-
-    total = head_mid[...] + dot_nt(
-        jnp.concatenate([head_edge_taps(f) for f in range(8)], axis=1),
-        jnp.concatenate([head_edges(f) for f in range(8)], axis=1),
-    )
+        if group == 1:
+            head_mid[...] += head_part(range(6))
+
+    total = head_mid[...] + head_part(range(6, 8))
     part = dot_nt(
         jnp.concatenate([edge_grads(0, late), edge_grads(1, late)], axis=0), edge_windows(late)
     )
@@ -509,23 +514,30 @@
     def pair_copy(c):
         return remote(piece[1 - c], got1[1 - c], s1, r1, sibling)
 
-    def scatter_copy(c, k):
-        part = sum1[c].at[chip_at(k)]
-        return remote(part, got2[c].at[k], s2, r2, in_plane(k))
-
-    def z_copy(c):
-        return remote(half3[c], got3[c], s3, r3, zpartner)
-
-    def gather_copy(c, k):
-        mine = full[c].at[xy]
-        return remote(mine, mine, s4, r4.at[k // 4], in_plane(k))
-
-    def pass_on(c, k):
-        one = full[c].at[chip_from(k)]
+    def parts_of(c):
+        rows = 16 * len(tiles_of(c)) // planes
+        cut = (rows // 16 + 1) // 2 * 16
+        return [span for span in (pl.ds(0, cut), pl.ds(cut, rows - cut)) if span.size]
+
+    def scatter_copy(c, k, n):
+        span = parts_of(c)[n]
+        there = got2[c].at[k, span]
+        return remote(sum1[c].at[chip_at(k), span], there, s2.at[n], r2.at[n], in_plane(k))
+
+    def z_copy(c, n):
+        span = parts_of(c)[n]
+        return remote(half3[c].at[span], got3[c].at[span], s3.at[n], r3.at[n], zpartner)
+
+    def gather_copy(c, k, n):
+        mine = full[c].at[xy, parts_of(c)[n]]
+        return remote(mine, mine, s4.at[n], r4.at[n, k // 4], in_plane(k))
+
+    def pass_on(c, k, n):
+        one = full[c].at[chip_from(k), parts_of(c)[n]]
         return remote(one, one, s5, r5, sibling)
 
-    def others(c):
-        return got2[c].at[pl.ds(1, planes - 1)]
+    def others(c, n, low=1, high=planes):
+        return got2[c].at[pl.ds(low, high - low), parts_of(c)[n]]
 
     def on_core(stage):
         for c in range(2):
@@ -546,35 +558,42 @@
             if tile < 126:
                 value = value + tile_of(tile)
             sum1[c][owner, rows] = value.astype(BF16)
-        for k in range(1, planes):
-            scatter_copy(c, k).start()
+        for n in range(len(parts_of(c))):
+            for k in range(1, planes):
+                scatter_copy(c, k, n).start()
 
     def start_z(c):
-        whole(others(c), s2, r2).wait_recv()
-        total = sum1[c][xy].astype(F32)
-        for k in range(1, planes):
-            total = total + got2[c][k].astype(F32)
-        half3[c][...] = total.astype(BF16)
-        z_copy(c).start()
+        for n, span in enumerate(parts_of(c)):
+            whole(others(c, n), s2.at[n], r2.at[n]).wait_recv()
+            total = sum1[c][xy, span].astype(F32)
+            for k in range(1, planes):
+                total = total + got2[c][k, span].astype(F32)
+            half3[c][span] = total.astype(BF16)
+            z_copy(c, n).start()
 
     def gather(c):
-        z_copy(c).wait_recv()
-        full[c][xy] = (half3[c][...].astype(F32) + got3[c][...].astype(F32)).astype(BF16)
-        for k in range(1, planes):
-            gather_copy(c, k).start()
-        pass_on(c, 0).start()
-        for low in range(0, planes, 4):
-            some = range(max(low, 1), min(low + 4, planes))
-            whole(got2[c].at[pl.ds(0, len(some))], s4, r4.at[low // 4]).wait_recv()
-            for k in some:
-                pass_on(c, k).start()
+        for n, span in enumerate(parts_of(c)):
+            z_copy(c, n).wait_recv()
+            both = half3[c][span].astype(F32) + got3[c][span].astype(F32)
+            full[c][xy, span] = both.astype(BF16)
+            for k in range(1, planes):
+                gather_copy(c, k, n).start()
+            pass_on(c, 0, n).start()
+        for n in range(len(parts_of(c))):
+            for low in range(0, planes, 4):
+                some = range(max(low, 1), min(low + 4, planes))
+                arrived = others(c, n, 0, len(some))
+                whole(arrived, s4.at[n], r4.at[n, low // 4]).wait_recv()
+                for k in some:
+                    pass_on(c, k, n).start()
         whole(full[1 - c], s5, r5).wait_recv()
 
     def sums_left(c):
         pair_copy(c).wait_send()
-        whole(others(c), s2, r2).wait_send()
-        z_copy(c).wait_send()
-        whole(others(c), s4, r4.at[0]).wait_send()
+        for n in range(len(parts_of(c))):
+            whole(others(c, n), s2.at[n], r2.at[n]).wait_send()
+            z_copy(c, n).wait_send()
+            whole(others(c, n), s4.at[n], r4.at[n, 0]).wait_send()
         whole(full[c], s5, r5).wait_send()
 
     on_core(start_pair)
@@ -732,12 +751,12 @@
             dma((2,)),
             dma,
             dma,
-            dma,
-            dma,
-            dma,
-            dma,
-            dma,
-            dma(((planes + 3) // 4,)),
+            dma((2,)),
+            dma((2,)),
+            dma((2,)),
+            dma((2,)),
+            dma((2,)),
+            dma((2, (planes + 3) // 4)),
             dma,
             dma,
         ],

time: 44.2 us -> 43.5 us (0.984)
  Pallas kernels: 43.3 us -> 42.3 us
    pallas_call x1, Pallas kernels: 41.8 us -> 40.9 us  [local(): pl.pallas_call(functools.partial(kernel, slabs), out_shape=(pltpu.VMEM(gi...]
where the time goes in v5:
time: 43.5 us; the launch traced here: 43 us
  Pallas kernels  42.3 us (97%)
  between operations  0.64 us (1%)
    pallas_call x1, Pallas kernels, local(): pl.pallas_call(functools.partial(kernel, slabs), out_shape=(pltpu.VMEM(gi...  40.9 us
    pallas_call x1, Pallas kernels, local(): pl.pallas_call(functools.partial(finish, slabs), out_shape=(gi_shape, jax...  1.49 us

profile of v5, /device:TPU:1, one launch (start us, length us, event | category | flops | bytes accessed | tf_op | source)
XLA Modules:
  0.0 43.0 jit_solution(14383714730077950667)
XLA Ops:
  0.6 40.9 %shard_map.130 = (f32[6,384,128]{2,1,0:T(8,128)S(1)}, bf16[16,16,128]{2,1,0:T(8,128)(2,1)S(1)}, bf16[16,112,128]{2,1,0:T(8,128)(2,1)S(1)}) custom-call(bf16[6,384,128]{2,1,0:T(8,128)(2,1)} %bitcast.7, bf16[2,384,128]{2,1,0:T(8,128)(2,1)} %bitcast.8, bf16[2,384,128]{2,1,0:T(8,128)(2,1)} %bitcast.9, f32[1,96]{1,0:T(1,128)} %bitcast.11, f32[1,96]{1,0:T(1,128)} %bitcast.12, ...), custom_call_target="tpu_custom_call" | custom-call | tf_op jit(solution)/shard_map/pallas_call | solution.py:708
  41.5 1.5 %shard_map.131 = (f32[6,384,128]{2,1,0:T(8,128)}, f32[3,3,3,96,96]{4,3,2,1,0:T(8,128)}, f32[3,3,3,3,96]{4,3,2,1,0:T(4,128)}) custom-call(f32[6,384,128]{2,1,0:T(8,128)S(1)} %get-tuple-element.9.gi_ref, bf16[16,16,128]{2,1,0:T(8,128)(2,1)S(1)} %get-tuple-element.10.sums0, bf16[16,112,128]{2,1,0:T(8,128)(2,1)S(1)} %get-tuple-element.11.sums1), custom_call_target="tpu_custom_call" | custom-call | tf_op jit(solution)/shard_map/pallas_call | solution.py:767

commit v6 on v5

--- a/solution.py
+++ b/solution.py
@@ -270,9 +270,15 @@
         return remote(row, there, ds.at[1], dr.at[0], down)
 
     pl.semaphore_wait(barrier, planes + 2)
-    for j in range(2):
-        for side in range(2):
-            hin_copy(side, j).start()
+    def halo(far, frames):
+        for c in range(2):
+
+            @pl.when(core == c)
+            def _():
+                for f in frames:
+                    hin_copy(c if far else 1 - c, f).start()
+
+    halo(True, range(2))
 
     for n in (7, 8, 9, 10):
         loads[n].wait()
@@ -305,11 +311,12 @@
         xs[f] = value
         _, _, normed, sig = norm_parts(value, wide(gains[0], 4 * COLS))
         hin[f + 2] = (normed * sig).astype(BF16)
-        for side in range(2):
-            hin_copy(side, f + 2).start()
 
     for f in range(0, FR):
         make_h(f)
+        if f % 2 == 1:
+            halo(True, range(f + 1, f + 3))
+    halo(False, range(8))
 
     loads[4].wait()
     gains[1] = jnp.broadcast_to(gout_ref[...], (COLS, C)).T
@@ -653,8 +660,9 @@
 
 
 def finish(slabs, gi_ref, sums0, sums1, out_hbm, gm_hbm, gh_hbm, grads, gm, gh, outs):
-    gi_out = pltpu.make_async_copy(gi_ref, out_hbm, outs.at[3])
-    gi_out.start()
+    gi_out = pltpu.make_async_copy(gi_ref, out_hbm, outs.at[0])
+    for f in range(FR):
+        pltpu.make_async_copy(gi_ref.at[f], out_hbm.at[f], outs.at[0]).start()
     planes = slabs // 4
     scale = (1.0 / (FR * slabs * 4 * COLS)) ** 0.5
     for c, sums in enumerate((sums0, sums1)):
@@ -664,23 +672,22 @@
                 row, lane = divmod(tile, 7)
                 value = sums[owner, rows].astype(F32) * scale
                 grads[row * 16 : (row + 1) * 16, lane * COLS : (lane + 1) * COLS] = value
-    gm_out = []
+    gm_out = pltpu.make_async_copy(gm, gm_hbm, outs.at[1])
     for t in range(3):
         for y in range(3):
             for x in range(3):
                 at = (y * 3 + t) * C
                 gm[t, y, x] = grads[x * C : (x + 1) * C, at : at + C]
-        gm_out.append(pltpu.make_async_copy(gm.at[t], gm_hbm.at[t], outs.at[t]))
-        gm_out[t].start()
+            pltpu.make_async_copy(gm.at[t, y], gm_hbm.at[t, y], outs.at[1]).start()
     head = jnp.concatenate([grads[n * C : (n + 1) * C, K3 : K3 + 32] for n in range(3)], axis=1)
     for y in range(3):
         for x in range(3):
             for t in range(3):
                 at = y * 32 + x * 9 + t * 3
                 gh[2 - t, y, x] = head[at : at + 3, :]
-    gh_out = pltpu.make_async_copy(gh, gh_hbm, outs.at[4])
+    gh_out = pltpu.make_async_copy(gh, gh_hbm, outs.at[2])
     gh_out.start()
-    for copy in [gi_out, gh_out] + gm_out:
+    for copy in (gi_out, gm_out, gh_out):
         copy.wait()
 
 
@@ -777,7 +784,7 @@
             pltpu.VMEM((3 * C, 7 * COLS), F32),
             pltpu.VMEM((3, 3, 3, C, C), F32),
             pltpu.VMEM((3, 3, 3, 3, C), F32),
-            dma((5,)),
+            dma((3,)),
         ],
         compiler_params=pltpu.CompilerParams(vmem_limit_bytes=16 * 2**20),
     )(gi, sums0, sums1)

time: 43.5 us -> 43.4 us (level)
  no operation moved by 1% of the time
where the time goes in v6:
time: 43.4 us; the launch traced here: 43 us
  Pallas kernels  42.3 us (97%)
  between operations  0.64 us (1%)
    pallas_call x1, Pallas kernels, local(): pl.pallas_call(functools.partial(kernel, slabs), out_shape=(pltpu.VMEM(gi...  40.9 us
    pallas_call x1, Pallas kernels, local(): pl.pallas_call(functools.partial(finish, slabs), out_shape=(gi_shape, jax...  1.47 us

profile of v6, /device:TPU:1, one launch (start us, length us, event | category | flops | bytes accessed | tf_op | source)
XLA Modules:
  0.0 43.0 jit_solution(5231686997165966381)
XLA Ops:
  0.6 40.9 %shard_map.130 = (f32[6,384,128]{2,1,0:T(8,128)S(1)}, bf16[16,16,128]{2,1,0:T(8,128)(2,1)S(1)}, bf16[16,112,128]{2,1,0:T(8,128)(2,1)S(1)}) custom-call(bf16[6,384,128]{2,1,0:T(8,128)(2,1)} %bitcast.7, bf16[2,384,128]{2,1,0:T(8,128)(2,1)} %bitcast.8, bf16[2,384,128]{2,1,0:T(8,128)(2,1)} %bitcast.9, f32[1,96]{1,0:T(1,128)} %bitcast.11, f32[1,96]{1,0:T(1,128)} %bitcast.12, ...), custom_call_target="tpu_custom_call" | custom-call | tf_op jit(solution)/shard_map/pallas_call | solution.py:715
  41.5 1.5 %shard_map.131 = (f32[6,384,128]{2,1,0:T(8,128)}, f32[3,3,3,96,96]{4,3,2,1,0:T(8,128)}, f32[3,3,3,3,96]{4,3,2,1,0:T(4,128)}) custom-call(f32[6,384,128]{2,1,0:T(8,128)S(1)} %get-tuple-element.9.gi_ref, bf16[16,16,128]{2,1,0:T(8,128)(2,1)S(1)} %get-tuple-element.10.sums0, bf16[16,112,128]{2,1,0:T(8,128)(2,1)S(1)} %get-tuple-element.11.sums1), custom_call_target="tpu_custom_call" | custom-call | tf_op jit(solution)/shard_map/pallas_call | solution.py:774
